TPU v7x, 512 devices: a whole 4x8x8 slice. The times are simulated.
512 devices in a mesh: pipe: 16 (over z_hi, x), ctx: 32 (over y, z_lo, core).
Axes of the slice: x: 4, y: 8, z: 8 (z_hi: 4, z_lo: 2; z = z_hi * 2 + z_lo), core: 2. Of those that a mesh axis runs over, the one named last changes fastest.
Arguments:
- queries: bfloat16 [16, 4096, 4096], P('pipe', 'ctx'), may hold values from -32 to 32
- keys: bfloat16 [16, 4096, 512], P('pipe', 'ctx'), may hold values from -32 to 32
- values: bfloat16 [16, 4096, 512], P('pipe', 'ctx'), may hold values from -6 to 6
- out_grad: bfloat16 [16, 4096, 4096], P('pipe', 'ctx'), may hold values from -6 to 6
- doc_ids: int32 [16, 4096], P('pipe', 'ctx'), may hold values from 0 to 15, never falling along the last dimension, each value on 1 to 512 neighbouring positions
Outputs:
- received_acts: bfloat16 [16, 4096, 4096], P('pipe', 'ctx')
- received_dq: bfloat16 [16, 4096, 4096], P('pipe', 'ctx')
- key_grads: bfloat16 [16, 4096, 512], P('pipe', 'ctx')
- value_grads: bfloat16 [16, 4096, 512], P('pipe', 'ctx')
Inputs may be any that keep to these rules, and one draw needn't show every extreme that they name: `doc_ids`: along each section's sequence the ids never fall; every id from 0 to 15 names one run of 1 to 512 consecutive tokens, and some run has exactly 512 tokens.
All inputs are finite; a program needn't handle non-finite values.
Results may differ from a plain program's by a relative error of at most 0.039.
The roundings to bfloat16 on the way count: a program that leaves them out, or rounds other values in their place, can miss the bound.
Values may be sent and summed in bfloat16 or wider, within the bound.
No kernel may reach another device: no remote copies, remote signals or barrier semaphores. Data moves between devices by JAX's collectives and lax.ppermute only.
A program may use at most 128 MiB of HBM per device.

v0:
```python
import jax
import jax.numpy as jnp
from jax import lax
from jax.sharding import PartitionSpec as P

HK = 4
DH = 128
REACH = 4
GROUP = 8


def passed_along(block, axis, distance):
    devices = range(lax.axis_size(axis))
    route = [(i - distance, i) for i in devices if i - distance in devices]
    return lax.ppermute(block, axis, route)


def attend(q_part, k_part, v_part, d_part, q_mark, k_mark, q_pos, k_pos):
    row_count = q_part.shape[0]
    q_heads = q_part.reshape(row_count, GROUP, DH)
    d_heads = d_part.reshape(row_count, GROUP, DH)
    scaling = DH ** (-0.5)
    visible = (q_mark[:, None] == k_mark[None, :]) & (k_pos[None, :] <= q_pos[:, None])
    scores = (
        jnp.einsum("thd,ud->htu", q_heads, k_part, preferred_element_type=jnp.float32) * scaling
    )
    scores = jnp.where(visible, scores, -1e30)
    row_max = jnp.max(scores, axis=-1, keepdims=True)
    raised = jnp.where(visible, jnp.exp(scores - row_max), 0.0)
    summed = jnp.sum(raised, axis=-1, keepdims=True)
    weights = raised / summed
    weights_b = weights.astype(jnp.bfloat16)
    attended = jnp.einsum(
        "htu,ud->thd", weights_b, v_part, preferred_element_type=jnp.float32
    ).astype(jnp.bfloat16)
    grad_weights = jnp.einsum("thd,ud->htu", d_heads, v_part, preferred_element_type=jnp.float32)
    row_delta = jnp.einsum("thd,thd->ht", d_heads, attended, preferred_element_type=jnp.float32)
    grad_scores = (weights * (grad_weights - row_delta[:, :, None])).astype(jnp.bfloat16)
    grad_q = (
        jnp.einsum("htu,ud->thd", grad_scores, k_part, preferred_element_type=jnp.float32) * scaling
    ).astype(jnp.bfloat16)
    grad_k = (
        jnp.einsum("htu,thd->ud", grad_scores, q_heads, preferred_element_type=jnp.float32)
        * scaling
    )
    grad_v = jnp.einsum("htu,thd->ud", weights_b, d_heads, preferred_element_type=jnp.float32)
    log_total = row_max[:, :, 0] + jnp.log(summed[:, :, 0])
    return (
        attended.reshape(row_count, GROUP * DH),
        grad_q.reshape(row_count, GROUP * DH),
        grad_k,
        grad_v,
        log_total,
        row_delta,
    )


def body(queries, keys, values, out_grad, doc_ids):
    q_rows = queries[0]
    k_rows = keys[0]
    v_rows = values[0]
    d_rows = out_grad[0]
    shard_rows = q_rows.shape[0]
    shard_index = lax.axis_index("ctx")
    doc_marks = doc_ids[0] + 1
    q_pos = shard_index * shard_rows + jnp.arange(shard_rows, dtype=jnp.int32)
    kv_width = HK * DH
    kv_pairs = jnp.concatenate([k_rows, v_rows], axis=1)
    pieces = []
    piece_marks = []
    for distance in range(REACH, 0, -1):
        got_pairs, got_marks = passed_along((kv_pairs, doc_marks), "ctx", distance)
        pieces.append(got_pairs)
        piece_marks.append(got_marks)
    pieces.append(kv_pairs)
    piece_marks.append(doc_marks)
    window = jnp.concatenate(pieces, axis=0)
    k_mark = jnp.concatenate(piece_marks, axis=0)
    key_count = window.shape[0]
    k_pos = (shard_index - REACH) * shard_rows + jnp.arange(key_count, dtype=jnp.int32)
    group_width = GROUP * DH
    attn_parts = []
    dq_parts = []
    dk_parts = []
    dv_parts = []
    log_parts = []
    delta_parts = []
    for head_group in range(HK):
        q_cols = slice(head_group * group_width, (head_group + 1) * group_width)
        k_cols = slice(head_group * DH, (head_group + 1) * DH)
        v_cols = slice(kv_width + head_group * DH, kv_width + (head_group + 1) * DH)
        attended, grad_q, grad_k, grad_v, log_total, row_delta = attend(
            q_rows[:, q_cols],
            window[:, k_cols],
            window[:, v_cols],
            d_rows[:, q_cols],
            doc_marks,
            k_mark,
            q_pos,
            k_pos,
        )
        attn_parts.append(attended)
        dq_parts.append(grad_q)
        dk_parts.append(grad_k)
        dv_parts.append(grad_v)
        log_parts.append(log_total)
        delta_parts.append(row_delta)
    attn_all = jnp.concatenate(attn_parts, axis=1)
    dq_all = jnp.concatenate(dq_parts, axis=1)
    grads_win = jnp.concatenate(dk_parts + dv_parts, axis=1)
    summed = grads_win[REACH * shard_rows :]
    for distance in range(1, REACH + 1):
        first_row = (REACH - distance) * shard_rows
        summed = summed + passed_along(
            grads_win[first_row : first_row + shard_rows], "ctx", -distance
        )
    kv_grads = summed.astype(jnp.bfloat16)
    acts_in = passed_along(attn_all, "pipe", 1)
    dq_in = passed_along(dq_all, "pipe", -1)
    return (acts_in[None], dq_in[None], kv_grads[None, :, :kv_width], kv_grads[None, :, kv_width:])


def solution(mesh):
    in_specs = (
        P("pipe", "ctx", None),
        P("pipe", "ctx", None),
        P("pipe", "ctx", None),
        P("pipe", "ctx", None),
        P("pipe", "ctx"),
    )
    out_specs = (
        P("pipe", "ctx", None),
        P("pipe", "ctx", None),
        P("pipe", "ctx", None),
        P("pipe", "ctx", None),
    )
    return jax.shard_map(body, mesh=mesh, in_specs=in_specs, out_specs=out_specs, check_vma=False)
```

profile of v0, /device:TPU:409, one launch (start us, length us, event | category | flops | bytes accessed | tf_op | source)
XLA Modules:
  0.0 203.1 jit_solution(6686882806476941641)
XLA Ops:
  1.3 3.6 %collective-permute-start.7 = (s32[128]{0:T(128)S(1)}, s32[128]{0:T(128)S(1)}, u32[]{:S(2)}, u32[]{:S(2)}) collective-permute-start(s32[128]{0:T(128)S(1)} %add_bitcast_fusion), channel_id=1, source_target_pairs={{0,1},{1,2},{2,3},{3,4},{4,5},{5,6},{6,7},{7,8},{8,9},{9,10},{10,1... | collective-permute-start | bytes 1544 | tf_op jit(solution)/shard_map/ppermute | solution.py:15
  4.9 4.4 %collective-permute-start.6 = (s32[128]{0:T(128)S(1)}, s32[128]{0:T(128)S(1)}, u32[]{:S(2)}, u32[]{:S(2)}) collective-permute-start(s32[128]{0:T(128)S(1)} %add_bitcast_fusion), channel_id=1, source_target_pairs={{0,2},{1,3},{2,4},{3,5},{4,6},{5,7},{6,8},{7,9},{8,10},{9,11},{10,... | collective-permute-start | bytes 1544 | tf_op jit(solution)/shard_map/ppermute | solution.py:15
  9.4 2.2 %collective-permute-start.5 = (s32[128]{0:T(128)S(1)}, s32[128]{0:T(128)S(1)}, u32[]{:S(2)}, u32[]{:S(2)}) collective-permute-start(s32[128]{0:T(128)S(1)} %add_bitcast_fusion), channel_id=1, source_target_pairs={{0,3},{1,4},{2,5},{3,6},{4,7},{5,8},{6,9},{7,10},{8,11},{9,12},{10... | collective-permute-start | bytes 1544 | tf_op jit(solution)/shard_map/ppermute | solution.py:15
  11.6 2.3 %collective-permute-start.4 = (s32[128]{0:T(128)S(1)}, s32[128]{0:T(128)S(1)}, u32[]{:S(2)}, u32[]{:S(2)}) collective-permute-start(s32[128]{0:T(128)S(1)} %add_bitcast_fusion), channel_id=1, source_target_pairs={{0,4},{1,5},{2,6},{3,7},{4,8},{5,9},{6,10},{7,11},{8,12},{9,13},{1... | collective-permute-start | bytes 1544 | tf_op jit(solution)/shard_map/ppermute | solution.py:15
  15.6 3.7 %collective-permute-start.3 = (bf16[128,1024]{1,0:T(8,128)(2,1)}, bf16[128,1024]{1,0:T(8,128)(2,1)}, u32[]{:S(2)}, u32[]{:S(2)}) collective-permute-start(bf16[128,1024]{1,0:T(8,128)(2,1)} %pad_maximum_fusion.2), channel_id=1, source_target_pairs={{0,1},{1,2},{2,3},{3,4},{4,5},{5,6},{6,7},{7,8},{8,9},{9,10},{10,1... | collective-permute-start | bytes 786440 | tf_op jit(solution)/shard_map/ppermute | solution.py:15
  23.2 3.1 %collective-permute-start.2 = (bf16[128,1024]{1,0:T(8,128)(2,1)}, bf16[128,1024]{1,0:T(8,128)(2,1)S(1)}, u32[]{:S(2)}, u32[]{:S(2)}) collective-permute-start(bf16[128,1024]{1,0:T(8,128)(2,1)} %pad_maximum_fusion.2), channel_id=1, source_target_pairs={{0,2},{1,3},{2,4},{3,5},{4,6},{5,7},{6,8},{7,9},{8,10},{9,11},{10,... | collective-permute-start | bytes 786440 | tf_op jit(solution)/shard_map/ppermute | solution.py:15
  28.3 2.3 %collective-permute-start = (bf16[128,1024]{1,0:T(8,128)(2,1)}, bf16[128,1024]{1,0:T(8,128)(2,1)S(1)}, u32[]{:S(2)}, u32[]{:S(2)}) collective-permute-start(bf16[128,1024]{1,0:T(8,128)(2,1)} %pad_maximum_fusion.2), channel_id=1, source_target_pairs={{0,4},{1,5},{2,6},{3,7},{4,8},{5,9},{6,10},{7,11},{8,12},{9,13},{1... | collective-permute-start | bytes 786440 | tf_op jit(solution)/shard_map/ppermute | solution.py:15
  30.9 7.5 %collective-permute-done = bf16[128,1024]{1,0:T(8,128)(2,1)S(1)} collective-permute-done((bf16[128,1024]{1,0:T(8,128)(2,1)}, bf16[128,1024]{1,0:T(8,128)(2,1)S(1)}, u32[]{:S(2)}, u32[]{:S(2)}) %collective-permute-start) | collective-permute-done | bytes 262176 | tf_op jit(solution)/shard_map/ppermute | solution.py:15
  41.2 2.7 %fusion.78 = (f32[8,128]{1,0:T(8,128)S(1)}, f32[8,128,640]{1,2,0:T(8,128)}) fusion(pred[128,640]{0,1:T(8,128)(4,1)S(1)} %compare_and_fusion, bf16[128,8,128]{0,2,1:T(8,128)(2,1)S(1)} %bitcast.277, bf16[640,1024]{1,0:T(8,128)(2,1)S(1)} %constant_dynamic-update-slice_fusion), kind=kOutput, calls=%fused_computation.138 | convolution fusion | flops 171049600 | bytes 3215360 | tf_op jit(solution)/shard_map/sub | solution.py:29
  46.2 2.6 %fusion.81 = (f32[8,128]{1,0:T(8,128)S(1)}, f32[8,128,640]{1,2,0:T(8,128)}) fusion(pred[128,640]{0,1:T(8,128)(4,1)S(1)} %compare_and_fusion, bf16[128,8,128]{0,2,1:T(8,128)(2,1)S(1)} %bitcast.283, bf16[640,1024]{1,0:T(8,128)(2,1)S(1)} %constant_dynamic-update-slice_fusion), kind=kOutput, calls=%fused_computation.141 | convolution fusion | flops 171049600 | bytes 3215360 | tf_op jit(solution)/shard_map/sub | solution.py:29
  48.9 2.0 fusion.44
  52.4 2.6 %fusion.79 = (f32[8,128]{1,0:T(8,128)S(1)}, f32[8,128,640]{1,2,0:T(8,128)}) fusion(pred[128,640]{0,1:T(8,128)(4,1)S(1)} %compare_and_fusion, bf16[128,8,128]{0,2,1:T(8,128)(2,1)S(1)} %bitcast.279, bf16[640,1024]{1,0:T(8,128)(2,1)S(1)} %constant_dynamic-update-slice_fusion), kind=kOutput, calls=%fused_computation.139 | convolution fusion | flops 171049600 | bytes 3215360 | tf_op jit(solution)/shard_map/sub | solution.py:29
  58.3 3.6 %fusion.80 = (f32[8,128]{1,0:T(8,128)S(1)}, f32[8,128,640]{1,2,0:T(8,128)}) fusion(pred[128,640]{0,1:T(8,128)(4,1)S(1)} %compare_and_fusion, bf16[128,8,128]{0,2,1:T(8,128)(2,1)} %bitcast.281, bf16[640,1024]{1,0:T(8,128)(2,1)} %copy-done.13), kind=kOutput, calls=%fused_computation.140 | convolution fusion | flops 171049600 | bytes 3215360 | tf_op jit(solution)/shard_map/sub | solution.py:29
  61.9 2.0 %fusion.45 = bf16[8,128,640]{1,2,0:T(8,128)(2,1)S(1)} fusion(f32[8,128,640]{1,2,0:T(8,128)} %get-tuple-element.41, f32[8,128]{1,0:T(8,128)S(1)} %get-tuple-element.40), kind=kLoop, calls=%fused_computation.77 | loop fusion | flops 1310720 | bytes 3936256 | tf_op jit(solution)/shard_map/convert_element_type | solution.py:32
  68.5 2.0 fusion.28
  73.6 2.4 %fusion.5 = bf16[8,128,640]{1,2,0:T(8,128)(2,1)S(1)} fusion(bf16[128,8,128]{0,2,1:T(8,128)(2,1)} %bitcast.269, f32[8,128]{1,0:T(8,128)S(1)} %get-tuple-element.24, f32[8,128,640]{1,2,0:T(8,128)} %get-tuple-element.37, f32[8,128]{1,0:T(8,128)S(1)} %get-tuple-element.36, bf16[640,1024]{1,0:T(8,128)(2,1)} %copy-done.13), kind=kOutput, calls=%fused_computation.6 | convolution fusion | flops 170393600 | bytes 4366336 | tf_op jit(solution)/shard_map/thd,ud->htu/dot_general | solution.py:36
  77.2 2.0 fusion.31
  81.0 2.6 %fusion.7 = bf16[8,128,640]{1,2,0:T(8,128)(2,1)S(1)} fusion(bf16[128,8,128]{0,2,1:T(8,128)(2,1)} %bitcast.271, f32[8,128]{1,0:T(8,128)S(1)} %get-tuple-element.26, f32[8,128,640]{1,2,0:T(8,128)} %get-tuple-element.39, f32[8,128]{1,0:T(8,128)S(1)} %get-tuple-element.38, bf16[640,1024]{1,0:T(8,128)(2,1)} %copy-done.13), kind=kOutput, calls=%fused_computation.9 | convolution fusion | flops 170393600 | bytes 4366336 | tf_op jit(solution)/shard_map/thd,ud->htu/dot_general | solution.py:36
  83.6 2.2 %fusion.30 = bf16[128,8,128]{2,0,1:T(8,128)(2,1)} fusion(bf16[8,128,640]{1,2,0:T(8,128)(2,1)S(1)} %fusion.7, bf16[640,1024]{1,0:T(8,128)(2,1)} %copy-done.13), kind=kOutput, calls=%fused_computation.50 | convolution fusion | flops 168034304 | bytes 1736704 | tf_op jit(solution)/shard_map/htu,ud->thd/dot_general | solution.py:40
  87.3 2.2 %fusion.29 = bf16[128,8,128]{2,0,1:T(8,128)(2,1)} fusion(bf16[8,128,640]{1,2,0:T(8,128)(2,1)S(1)} %fusion.9, bf16[640,1024]{1,0:T(8,128)(2,1)} %copy-done.13), kind=kOutput, calls=%fused_computation.49 | convolution fusion | flops 168034304 | bytes 1736704 | tf_op jit(solution)/shard_map/htu,ud->thd/dot_general | solution.py:40
  93.2 2.7 %fusion.41 = f32[640,1024]{0,1:T(8,128)} fusion(f32[640,1024]{0,1:T(8,128)} %fusion.43, bf16[8,128,640]{1,2,0:T(8,128)(2,1)} %copy-done.7, bf16[128,8,128]{0,2,1:T(8,128)(2,1)} %bitcast.282), kind=kOutput, calls=%fused_computation.72 | convolution fusion | flops 167854080 | bytes 1900544 | tf_op jit(solution)/shard_map/htu,thd->ud/dot_general | solution.py:43
  95.9 2.7 %fusion.39 = f32[640,1024]{0,1:T(8,128)} fusion(f32[640,1024]{0,1:T(8,128)} %fusion.41, bf16[8,128,640]{1,2,0:T(8,128)(2,1)} %copy-done.6, bf16[128,8,128]{0,2,1:T(8,128)(2,1)} %bitcast.280), kind=kOutput, calls=%fused_computation.69 | convolution fusion | flops 167854080 | bytes 1900544 | tf_op jit(solution)/shard_map/htu,thd->ud/dot_general | solution.py:43
  105.2 3.0 %fusion.76 = (f32[128,1024]{0,1:T(8,128)}, f32[128,1024]{0,1:T(8,128)}, f32[128,1024]{0,1:T(8,128)}, f32[128,1024]{0,1:T(8,128)}) fusion(f32[640,1024]{0,1:T(8,128)} %fusion.32), kind=kLoop, calls=%fused_computation.136 | loop fusion | bytes 4194304 | tf_op jit(solution)/shard_map/slice | solution.py:115
  108.2 2.0 %collective-permute-start.10 = (f32[128,1024]{0,1:T(8,128)}, f32[128,1024]{0,1:T(8,128)}, u32[]{:S(2)}, u32[]{:S(2)}) collective-permute-start(f32[128,1024]{0,1:T(8,128)} %get-tuple-element.20), channel_id=1, source_target_pairs={{1,0},{2,1},{3,2},{4,3},{5,4},{6,5},{7,6},{8,7},{9,8},{10,9},{11,1... | collective-permute-start | bytes 1572872 | tf_op jit(solution)/shard_map/ppermute | solution.py:15
  113.7 4.4 %collective-permute-start.9 = (bf16[128,4096]{1,0:T(8,128)(2,1)S(1)}, bf16[128,4096]{1,0:T(8,128)(2,1)S(1)}, u32[]{:S(2)}, u32[]{:S(2)}) collective-permute-start(bf16[128,4096]{1,0:T(8,128)(2,1)S(1)} %pad_maximum_fusion.1), channel_id=1, source_target_pairs={{32,0},{64,32},{96,64},{128,96},{160,128},{192,160},{224,192},{256... | collective-permute-start | bytes 3145736 | tf_op jit(solution)/shard_map/ppermute | solution.py:15
  118.1 3.0 %collective-permute-start.13 = (f32[128,1024]{0,1:T(8,128)}, f32[128,1024]{0,1:T(8,128)S(1)}, u32[]{:S(2)}, u32[]{:S(2)}) collective-permute-start(f32[128,1024]{0,1:T(8,128)} %get-tuple-element.21), channel_id=1, source_target_pairs={{4,0},{5,1},{6,2},{7,3},{8,4},{9,5},{10,6},{11,7},{12,8},{13,9},{1... | collective-permute-start | bytes 1572872 | tf_op jit(solution)/shard_map/ppermute | solution.py:15
  121.0 8.2 %collective-permute-start.12 = (f32[128,1024]{0,1:T(8,128)}, f32[128,1024]{0,1:T(8,128)S(1)}, u32[]{:S(2)}, u32[]{:S(2)}) collective-permute-start(f32[128,1024]{0,1:T(8,128)} %get-tuple-element.22), channel_id=1, source_target_pairs={{3,0},{4,1},{5,2},{6,3},{7,4},{8,5},{9,6},{10,7},{11,8},{12,9},{13... | collective-permute-start | bytes 1572872 | tf_op jit(solution)/shard_map/ppermute | solution.py:15
  129.3 2.2 %collective-permute-start.11 = (f32[128,1024]{0,1:T(8,128)}, f32[128,1024]{0,1:T(8,128)S(1)}, u32[]{:S(2)}, u32[]{:S(2)}) collective-permute-start(f32[128,1024]{0,1:T(8,128)} %get-tuple-element.23), channel_id=1, source_target_pairs={{2,0},{3,1},{4,2},{5,3},{6,4},{7,5},{8,6},{9,7},{10,8},{11,9},{12,... | collective-permute-start | bytes 1572872 | tf_op jit(solution)/shard_map/ppermute | solution.py:15
  134.7 17.7 %collective-permute-done.12 = f32[128,1024]{0,1:T(8,128)S(1)} collective-permute-done((f32[128,1024]{0,1:T(8,128)}, f32[128,1024]{0,1:T(8,128)S(1)}, u32[]{:S(2)}, u32[]{:S(2)}) %collective-permute-start.12) | collective-permute-done | bytes 524320 | tf_op jit(solution)/shard_map/ppermute | solution.py:15
  152.5 12.7 %collective-permute-done.11 = f32[128,1024]{0,1:T(8,128)S(1)} collective-permute-done((f32[128,1024]{0,1:T(8,128)}, f32[128,1024]{0,1:T(8,128)S(1)}, u32[]{:S(2)}, u32[]{:S(2)}) %collective-permute-start.11) | collective-permute-done | bytes 524320 | tf_op jit(solution)/shard_map/ppermute | solution.py:15
  168.1 31.8 %collective-permute-done.8 = bf16[128,4096]{1,0:T(8,128)(2,1)} collective-permute-done((bf16[128,4096]{1,0:T(8,128)(2,1)S(1)}, bf16[128,4096]{1,0:T(8,128)(2,1)}, u32[]{:S(2)}, u32[]{:S(2)}) %collective-permute-start.8) | collective-permute-done | bytes 1048608 | tf_op jit(solution)/shard_map/ppermute | solution.py:15
  199.8 2.3 %copy.181 = bf16[1,128,4096]{2,1,0:T(8,128)(2,1)} copy(bf16[1,128,4096]{2,1,0:T(8,128)(2,1)} %bitcast.36) | data formatting | bytes 2097152
  (127 shorter events, 50.9 us)
Async XLA Ops:
  1.3 29.3 %collective-permute-start.7 = (s32[128]{0:T(128)S(1)}, s32[128]{0:T(128)S(1)}, u32[]{:S(2)}, u32[]{:S(2)}) collective-permute-start(s32[128]{0:T(128)S(1)} %add_bitcast_fusion), channel_id=1, source_target_pairs={{0,1},{1,2},{2,3},{3,4},{4,5},{5,6},{6,7},{7,8},{8,9},{9,10},{10,1... | collective-permute-start | bytes 1544 | tf_op jit(solution)/shard_map/ppermute | solution.py:15
  4.9 23.3 %collective-permute-start.6 = (s32[128]{0:T(128)S(1)}, s32[128]{0:T(128)S(1)}, u32[]{:S(2)}, u32[]{:S(2)}) collective-permute-start(s32[128]{0:T(128)S(1)} %add_bitcast_fusion), channel_id=1, source_target_pairs={{0,2},{1,3},{2,4},{3,5},{4,6},{5,7},{6,8},{7,9},{8,10},{9,11},{10,... | collective-permute-start | bytes 1544 | tf_op jit(solution)/shard_map/ppermute | solution.py:15
  9.4 17.0 %collective-permute-start.5 = (s32[128]{0:T(128)S(1)}, s32[128]{0:T(128)S(1)}, u32[]{:S(2)}, u32[]{:S(2)}) collective-permute-start(s32[128]{0:T(128)S(1)} %add_bitcast_fusion), channel_id=1, source_target_pairs={{0,3},{1,4},{2,5},{3,6},{4,7},{5,8},{6,9},{7,10},{8,11},{9,12},{10... | collective-permute-start | bytes 1544 | tf_op jit(solution)/shard_map/ppermute | solution.py:15
  11.6 11.6 %collective-permute-start.4 = (s32[128]{0:T(128)S(1)}, s32[128]{0:T(128)S(1)}, u32[]{:S(2)}, u32[]{:S(2)}) collective-permute-start(s32[128]{0:T(128)S(1)} %add_bitcast_fusion), channel_id=1, source_target_pairs={{0,4},{1,5},{2,6},{3,7},{4,8},{5,9},{6,10},{7,11},{8,12},{9,13},{1... | collective-permute-start | bytes 1544 | tf_op jit(solution)/shard_map/ppermute | solution.py:15
  15.6 24.5 %collective-permute-start.3 = (bf16[128,1024]{1,0:T(8,128)(2,1)}, bf16[128,1024]{1,0:T(8,128)(2,1)}, u32[]{:S(2)}, u32[]{:S(2)}) collective-permute-start(bf16[128,1024]{1,0:T(8,128)(2,1)} %pad_maximum_fusion.2), channel_id=1, source_target_pairs={{0,1},{1,2},{2,3},{3,4},{4,5},{5,6},{6,7},{7,8},{8,9},{9,10},{10,1... | collective-permute-start | bytes 786440 | tf_op jit(solution)/shard_map/ppermute | solution.py:15
  21.1 9.6 %copy-start.32 = (s32[1,128]{1,0:T(1,128)S(1)}, s32[1,128]{1,0:T(1,128)}, u32[]{:S(2)}) copy-start(s32[1,128]{1,0:T(1,128)} %param.9) | copy-start | bytes 1540
  21.9 19.3 %copy-start.25 = (bf16[128,1024]{0,1:T(8,128)(2,1)}, bf16[128,1024]{0,1:T(8,128)(2,1)S(1)}, u32[]{:S(2)}) copy-start(bf16[128,1024]{0,1:T(8,128)(2,1)S(1)} %get-tuple-element.31) | copy-start | bytes 786436
  21.9 24.4 %copy-start.28 = (bf16[128,1024]{0,1:T(8,128)(2,1)}, bf16[128,1024]{0,1:T(8,128)(2,1)S(1)}, u32[]{:S(2)}) copy-start(bf16[128,1024]{0,1:T(8,128)(2,1)S(1)} %get-tuple-element.30) | copy-start | bytes 786436
  21.9 30.5 %copy-start.27 = (bf16[128,1024]{0,1:T(8,128)(2,1)}, bf16[128,1024]{0,1:T(8,128)(2,1)S(1)}, u32[]{:S(2)}) copy-start(bf16[128,1024]{0,1:T(8,128)(2,1)S(1)} %get-tuple-element.32) | copy-start | bytes 786436
  21.9 19.2 %copy-start.30 = (bf16[1,128,512]{2,1,0:T(8,128)(2,1)S(1)}, bf16[1,128,512]{2,1,0:T(8,128)(2,1)}, u32[]{:S(2)}) copy-start(bf16[1,128,512]{2,1,0:T(8,128)(2,1)} %param.7) | copy-start | bytes 393220
  21.9 19.2 %copy-start.31 = (bf16[1,128,512]{2,1,0:T(8,128)(2,1)S(1)}, bf16[1,128,512]{2,1,0:T(8,128)(2,1)}, u32[]{:S(2)}) copy-start(bf16[1,128,512]{2,1,0:T(8,128)(2,1)} %param.6) | copy-start | bytes 393220
  23.2 16.9 %collective-permute-start.2 = (bf16[128,1024]{1,0:T(8,128)(2,1)}, bf16[128,1024]{1,0:T(8,128)(2,1)S(1)}, u32[]{:S(2)}, u32[]{:S(2)}) collective-permute-start(bf16[128,1024]{1,0:T(8,128)(2,1)} %pad_maximum_fusion.2), channel_id=1, source_target_pairs={{0,2},{1,3},{2,4},{3,5},{4,6},{5,7},{6,8},{7,9},{8,10},{9,11},{10,... | collective-permute-start | bytes 786440 | tf_op jit(solution)/shard_map/ppermute | solution.py:15
  26.4 13.7 %collective-permute-start.1 = (bf16[128,1024]{1,0:T(8,128)(2,1)}, bf16[128,1024]{1,0:T(8,128)(2,1)S(1)}, u32[]{:S(2)}, u32[]{:S(2)}) collective-permute-start(bf16[128,1024]{1,0:T(8,128)(2,1)} %pad_maximum_fusion.2), channel_id=1, source_target_pairs={{0,3},{1,4},{2,5},{3,6},{4,7},{5,8},{6,9},{7,10},{8,11},{9,12},{10... | collective-permute-start | bytes 786440 | tf_op jit(solution)/shard_map/ppermute | solution.py:15
  28.3 10.1 %collective-permute-start = (bf16[128,1024]{1,0:T(8,128)(2,1)}, bf16[128,1024]{1,0:T(8,128)(2,1)S(1)}, u32[]{:S(2)}, u32[]{:S(2)}) collective-permute-start(bf16[128,1024]{1,0:T(8,128)(2,1)} %pad_maximum_fusion.2), channel_id=1, source_target_pairs={{0,4},{1,5},{2,6},{3,7},{4,8},{5,9},{6,10},{7,11},{8,12},{9,13},{1... | collective-permute-start | bytes 786440 | tf_op jit(solution)/shard_map/ppermute | solution.py:15
  41.2 11.2 %copy-start.13 = (bf16[640,1024]{1,0:T(8,128)(2,1)}, bf16[640,1024]{1,0:T(8,128)(2,1)S(1)}, u32[]{:S(2)}) copy-start(bf16[640,1024]{1,0:T(8,128)(2,1)S(1)} %constant_dynamic-update-slice_fusion) | copy-start | bytes 3932164
  81.0 4.8 %copy-start.9 = (f32[8,128,640]{1,2,0:T(8,128)S(1)}, f32[8,128,640]{1,2,0:T(8,128)}, u32[]{:S(2)}) copy-start(f32[8,128,640]{1,2,0:T(8,128)} %get-tuple-element.41) | copy-start | bytes 7864324
  81.0 4.8 %copy-start.17 = (bf16[128,1024]{0,1:T(8,128)(2,1)S(1)}, bf16[128,1024]{0,1:T(8,128)(2,1)}, u32[]{:S(2)}) copy-start(bf16[128,1024]{0,1:T(8,128)(2,1)} %get-tuple-element.29) | copy-start | bytes 786436
  93.2 5.5 %copy-start.5 = (bf16[8,128,640]{1,2,0:T(8,128)(2,1)S(1)}, bf16[8,128,640]{1,2,0:T(8,128)(2,1)}, u32[]{:S(2)}) copy-start(bf16[8,128,640]{1,2,0:T(8,128)(2,1)} %copy-done.4) | copy-start | bytes 3932164
  93.2 5.5 %copy-start.26 = (bf16[128,1024]{0,1:T(8,128)(2,1)S(1)}, bf16[128,1024]{0,1:T(8,128)(2,1)}, u32[]{:S(2)}) copy-start(bf16[128,1024]{0,1:T(8,128)(2,1)} %copy-done.25) | copy-start | bytes 786436
  95.9 4.2 %copy-start.1 = (bf16[8,128,640]{1,2,0:T(8,128)(2,1)S(1)}, bf16[8,128,640]{1,2,0:T(8,128)(2,1)}, u32[]{:S(2)}) copy-start(bf16[8,128,640]{1,2,0:T(8,128)(2,1)} %copy-done) | copy-start | bytes 3932164
  95.9 4.2 %copy-start.20 = (bf16[128,1024]{0,1:T(8,128)(2,1)S(1)}, bf16[128,1024]{0,1:T(8,128)(2,1)}, u32[]{:S(2)}) copy-start(bf16[128,1024]{0,1:T(8,128)(2,1)} %copy-done.19) | copy-start | bytes 786436
  105.2 5.0 %copy-start.21 = (bf16[128,1024]{1,0:T(8,128)(2,1)S(1)}, bf16[128,1024]{1,0:T(8,128)(2,1)}, u32[]{:S(2)}) copy-start(bf16[128,1024]{1,0:T(8,128)(2,1)} %copy.81) | copy-start | bytes 786436
  105.2 5.1 %copy-start.22 = (bf16[128,1024]{1,0:T(8,128)(2,1)S(1)}, bf16[128,1024]{1,0:T(8,128)(2,1)}, u32[]{:S(2)}) copy-start(bf16[128,1024]{1,0:T(8,128)(2,1)} %copy.84) | copy-start | bytes 786436
  105.2 5.1 %copy-start.23 = (bf16[128,1024]{1,0:T(8,128)(2,1)S(1)}, bf16[128,1024]{1,0:T(8,128)(2,1)}, u32[]{:S(2)}) copy-start(bf16[128,1024]{1,0:T(8,128)(2,1)} %copy.82) | copy-start | bytes 786436
  105.2 5.1 %copy-start.24 = (bf16[128,1024]{1,0:T(8,128)(2,1)S(1)}, bf16[128,1024]{1,0:T(8,128)(2,1)}, u32[]{:S(2)}) copy-start(bf16[128,1024]{1,0:T(8,128)(2,1)} %copy.83) | copy-start | bytes 786436
  108.2 4.7 %copy-start.12 = (bf16[128,8,128]{2,0,1:T(8,128)(2,1)S(1)}, bf16[128,8,128]{2,0,1:T(8,128)(2,1)}, u32[]{:S(2)}) copy-start(bf16[128,8,128]{2,0,1:T(8,128)(2,1)} %copy-done.11) | copy-start | bytes 786436
  108.2 24.6 %collective-permute-start.10 = (f32[128,1024]{0,1:T(8,128)}, f32[128,1024]{0,1:T(8,128)}, u32[]{:S(2)}, u32[]{:S(2)}) collective-permute-start(f32[128,1024]{0,1:T(8,128)} %get-tuple-element.20), channel_id=1, source_target_pairs={{1,0},{2,1},{3,2},{4,3},{5,4},{6,5},{7,6},{8,7},{9,8},{10,9},{11,1... | collective-permute-start | bytes 1572872 | tf_op jit(solution)/shard_map/ppermute | solution.py:15
  113.7 54.4 %collective-permute-start.9 = (bf16[128,4096]{1,0:T(8,128)(2,1)S(1)}, bf16[128,4096]{1,0:T(8,128)(2,1)S(1)}, u32[]{:S(2)}, u32[]{:S(2)}) collective-permute-start(bf16[128,4096]{1,0:T(8,128)(2,1)S(1)} %pad_maximum_fusion.1), channel_id=1, source_target_pairs={{32,0},{64,32},{96,64},{128,96},{160,128},{192,160},{224,192},{256... | collective-permute-start | bytes 3145736 | tf_op jit(solution)/shard_map/ppermute | solution.py:15
  118.1 16.7 %collective-permute-start.13 = (f32[128,1024]{0,1:T(8,128)}, f32[128,1024]{0,1:T(8,128)S(1)}, u32[]{:S(2)}, u32[]{:S(2)}) collective-permute-start(f32[128,1024]{0,1:T(8,128)} %get-tuple-element.21), channel_id=1, source_target_pairs={{4,0},{5,1},{6,2},{7,3},{8,4},{9,5},{10,6},{11,7},{12,8},{13,9},{1... | collective-permute-start | bytes 1572872 | tf_op jit(solution)/shard_map/ppermute | solution.py:15
  121.0 31.4 %collective-permute-start.12 = (f32[128,1024]{0,1:T(8,128)}, f32[128,1024]{0,1:T(8,128)S(1)}, u32[]{:S(2)}, u32[]{:S(2)}) collective-permute-start(f32[128,1024]{0,1:T(8,128)} %get-tuple-element.22), channel_id=1, source_target_pairs={{3,0},{4,1},{5,2},{6,3},{7,4},{8,5},{9,6},{10,7},{11,8},{12,9},{13... | collective-permute-start | bytes 1572872 | tf_op jit(solution)/shard_map/ppermute | solution.py:15
  129.3 35.9 %collective-permute-start.11 = (f32[128,1024]{0,1:T(8,128)}, f32[128,1024]{0,1:T(8,128)S(1)}, u32[]{:S(2)}, u32[]{:S(2)}) collective-permute-start(f32[128,1024]{0,1:T(8,128)} %get-tuple-element.23), channel_id=1, source_target_pairs={{2,0},{3,1},{4,2},{5,3},{6,4},{7,5},{8,6},{9,7},{10,8},{11,9},{12,... | collective-permute-start | bytes 1572872 | tf_op jit(solution)/shard_map/ppermute | solution.py:15
  132.8 67.0 %collective-permute-start.8 = (bf16[128,4096]{1,0:T(8,128)(2,1)S(1)}, bf16[128,4096]{1,0:T(8,128)(2,1)}, u32[]{:S(2)}, u32[]{:S(2)}) collective-permute-start(bf16[128,4096]{1,0:T(8,128)(2,1)S(1)} %pad_maximum_fusion), channel_id=1, source_target_pairs={{0,32},{32,64},{64,96},{96,128},{128,160},{160,192},{192,224},{224... | collective-permute-start | bytes 3145736 | tf_op jit(solution)/shard_map/ppermute | solution.py:15
  (15 other events, 37.5 us)
where the time goes:
time: 204 us; the launch traced here: 203 us
  waiting for transfers between devices  71.3 us (35%)
  starting transfers between devices  45.4 us (22%)
  matrix products  45 us (22%)
  local copies, waits for them, and re-layouts  25.6 us (13%)
  other arithmetic  14.5 us (7%)
    ppermute x14, waiting for transfers between devices, passed_along(): return lax.ppermute(block, axis, route)  71.3 us
    ppermute x14, starting transfers between devices, passed_along(): return lax.ppermute(block, axis, route)  45.4 us
    sub x4, matrix products, attend(): raised = jnp.where(visible, jnp.exp(scores - row_max), 0.0)  11.5 us
    unnamed x80, local copies, waits for them, and re-layouts  11.3 us
    dot_general x4, matrix products, attend(): jnp.einsum('htu,ud->thd', grad_scores, k_part, preferred_element_type=jnp...  8.51 us
    dot_general x4, matrix products, attend(): jnp.einsum('htu,thd->ud', grad_scores, q_heads, preferred_element_type=jn...  8.15 us
    dot_general x4, matrix products, attend(): jnp.einsum('thd,ud->htu', d_heads, v_part, preferred_element_type=jnp.flo...  7.99 us
    convert_element_type x4, other arithmetic, attend(): weights_b = weights.astype(jnp.bfloat16)  7.92 us
  transfers between devices with their start and end apart: 14, of which 5 were waited for; matrix products, arithmetic and copies ran while one was open for 7% of the time, Pallas kernels for 0%

commit v1 on v0

v1 whole, which is shorter than its diff:
```python
import jax
import jax.numpy as jnp
from jax import lax
from jax.experimental import pallas as pl
from jax.experimental.pallas import tpu as pltpu
from jax.sharding import PartitionSpec as P

HK = 4
DH = 128
GROUP = 8
ROWS = 128
PAIR = 2
MARK_ROWS = 16
SCALING = DH ** (-0.5)
LOG2E = 1.4426950408889634
F32 = jnp.float32
BF16 = jnp.bfloat16
NT = (((1,), (1,)), ((), ()))
NN = (((1,), (0,)), ((), ()))


def dot(a, b, dims=NN):
    return lax.dot_general(a, b, dims, preferred_element_type=F32)


def kernel(*refs):
    q_ref, d_ref = refs[:2]
    k_refs, v_refs, m_refs = refs[2:7], refs[7:12], refs[12:17]
    attn_ref, dq_ref = refs[17:19]
    g_refs = refs[19:24]
    bias, s_sc, p_sc, ds_sc = refs[24:28]
    u_pos = lax.broadcasted_iota(jnp.int32, (ROWS, ROWS), 0)
    t_pos = lax.broadcasted_iota(jnp.int32, (ROWS, ROWS), 1)
    tri = u_pos <= t_pos

    @pl.when(pl.program_id(0) == 0)
    def _():
        def col(ref):
            row = ref[0:1, :].astype(F32)
            return jnp.transpose(jnp.broadcast_to(row, (ROWS, ROWS)))

        q_mark = jnp.broadcast_to(m_refs[0][0:1, :].astype(F32), (ROWS, ROWS))
        marks = [jnp.where(tri, col(m_refs[0]), col(m_refs[1]))]
        marks += [col(m) for m in m_refs[2:]]
        for j, k_mark in enumerate(marks):
            bias[j] = jnp.where(k_mark == q_mark, 0.0, -1e30)

    ks = [k[...] for k in k_refs]
    vs = [v[...] for v in v_refs]
    k_t = jnp.concatenate([jnp.transpose(k) for k in ks], axis=1)
    v_t = jnp.concatenate([jnp.transpose(v) for v in vs], axis=1)
    width = PAIR * ROWS
    tri_w = jnp.concatenate([tri] * PAIR, axis=1)
    zero = jnp.zeros((ROWS, width), BF16)

    def merged(blocks):
        return [jnp.where(tri_w, blocks[0], blocks[1])] + list(blocks[2:])

    for unit in range(GROUP // PAIR):
        heads = range(unit * PAIR, (unit + 1) * PAIR)
        cols = slice(unit * width, (unit + 1) * width)
        q_t = jnp.concatenate(
            [jnp.transpose(q_ref[:, h * DH : (h + 1) * DH]) for h in heads], axis=1
        )
        d_t = jnp.concatenate(
            [jnp.transpose(d_ref[:, h * DH : (h + 1) * DH]) for h in heads], axis=1
        )
        scores = merged([dot(k, q_t) for k in ks])
        top = None
        for j, s in enumerate(scores):
            b = bias[j]
            s = s + jnp.concatenate([b] * PAIR, axis=1)
            s_sc[unit, j] = s
            m = jnp.max(s.reshape(ROWS // 8, 8, width), axis=0)
            top = m if top is None else jnp.maximum(top, m)
        top = jnp.max(top, axis=0, keepdims=True)
        total = None
        for j in range(4):
            e = jnp.exp2((s_sc[unit, j] - top) * (SCALING * LOG2E))
            s_sc[unit, j] = e
            part = jnp.sum(e.reshape(ROWS // 8, 8, width), axis=0)
            total = part if total is None else total + part
        inv = 1.0 / jnp.sum(total, axis=0, keepdims=True)
        for j in range(4):
            w = s_sc[unit, j] * inv
            s_sc[unit, j] = w
            wb = w.astype(BF16)
            if j == 0:
                p_sc[0, :, cols] = jnp.where(tri_w, wb, zero)
                p_sc[1, :, cols] = jnp.where(tri_w, zero, wb)
            else:
                p_sc[j + 1, :, cols] = wb
        p_all = p_sc[:, :, cols].reshape(5 * ROWS, width)
        att = dot(v_t, p_all).astype(BF16)
        delta = jnp.sum(d_t.astype(F32) * att.astype(F32), axis=0, keepdims=True)
        for i, h in enumerate(heads):
            attn_ref[:, h * DH : (h + 1) * DH] = jnp.transpose(att[:, i * ROWS : (i + 1) * ROWS])
        grads = merged([dot(v, d_t) for v in vs])
        for j, gw in enumerate(grads):
            ds = (s_sc[unit, j] * (gw - delta)).astype(BF16)
            if j == 0:
                ds_sc[0, :, cols] = jnp.where(tri_w, ds, zero)
                ds_sc[1, :, cols] = jnp.where(tri_w, zero, ds)
            else:
                ds_sc[j + 1, :, cols] = ds
        ds_all = ds_sc[:, :, cols].reshape(5 * ROWS, width)
        dq = (dot(k_t, ds_all) * SCALING).astype(BF16)
        for i, h in enumerate(heads):
            dq_ref[:, h * DH : (h + 1) * DH] = jnp.transpose(dq[:, i * ROWS : (i + 1) * ROWS])
    q_stack = jnp.concatenate([q_ref[:, h * DH : (h + 1) * DH] for h in range(GROUP)], axis=0)
    d_stack = jnp.concatenate([d_ref[:, h * DH : (h + 1) * DH] for h in range(GROUP)], axis=0)
    for j in range(5):
        g_refs[j][0, 0] = dot(ds_sc[j], q_stack) * SCALING
        g_refs[j][1, 0] = dot(p_sc[j], d_stack)


def attend(q_rows, d_rows, blocks, first, count):
    width = GROUP * DH
    wide = pl.BlockSpec((ROWS, width), lambda a: (0, first + a))
    wide_out = pl.BlockSpec((ROWS, width), lambda a: (0, a))
    k_spec = pl.BlockSpec((ROWS, DH), lambda a: (first + a, 0))
    v_spec = pl.BlockSpec((ROWS, DH), lambda a: (HK + first + a, 0))
    m_spec = pl.BlockSpec((MARK_ROWS, DH), lambda a: (2 * HK * ROWS // MARK_ROWS, 0))
    g_spec = pl.BlockSpec((2, 1, ROWS, DH), lambda a: (0, a, 0, 0))
    pairs = ROWS * ROWS * 5 * GROUP * count
    return pl.pallas_call(
        kernel,
        grid=(count,),
        in_specs=[wide] * 2 + [k_spec] * 5 + [v_spec] * 5 + [m_spec] * 5,
        out_specs=[wide_out] * 2 + [g_spec] * 5,
        out_shape=[jax.ShapeDtypeStruct((ROWS, count * width), BF16)] * 2
        + [jax.ShapeDtypeStruct((2, count, ROWS, DH), F32)] * 5,
        scratch_shapes=[
            pltpu.VMEM((4, ROWS, ROWS), F32),
            pltpu.VMEM((GROUP // PAIR, 4, ROWS, PAIR * ROWS), F32),
            pltpu.VMEM((5, ROWS, width), BF16),
            pltpu.VMEM((5, ROWS, width), BF16),
        ],
        compiler_params=pltpu.CompilerParams(vmem_limit_bytes=48 * 1024 * 1024),
        cost_estimate=pl.CostEstimate(
            flops=12 * DH * pairs, bytes_accessed=8 << 20, transcendentals=pairs
        ),
    )(q_rows, d_rows, *blocks, *blocks, *blocks)


REACH = 4
CHIP = 2
GROUP_SHARDS = 4
HALF = 2


def pack_kernel(k_ref, v_ref, m_ref, out_ref):
    for a in range(HK):
        cols = slice(a * DH, (a + 1) * DH)
        out_ref[a * ROWS : (a + 1) * ROWS, :] = k_ref[:, cols]
        out_ref[(HK + a) * ROWS : (HK + a + 1) * ROWS, :] = v_ref[:, cols]
    marks = (m_ref[...] + 1).astype(F32).astype(BF16)
    out_ref[2 * HK * ROWS :, :] = jnp.broadcast_to(marks, (MARK_ROWS, ROWS))


def pack(k_rows, v_rows, marks):
    return pl.pallas_call(
        pack_kernel,
        out_shape=jax.ShapeDtypeStruct((2 * HK * ROWS + MARK_ROWS, DH), BF16),
    )(k_rows, v_rows, marks)


def final_kernel(*refs):
    count = len(refs[:-2]) // 2
    for piece in range(count):
        total = refs[2 * piece][...] + refs[2 * piece + 1][...]
        for i in range(HALF):
            a = piece * HALF + i
            for out, which in ((refs[-2], 0), (refs[-1], 1)):
                out[:, a * DH : (a + 1) * DH] = total[which, i].astype(BF16)


def finish(parts):
    return pl.pallas_call(
        final_kernel,
        out_shape=[jax.ShapeDtypeStruct((ROWS, HK * DH), BF16)] * 2,
    )(*parts)


def swapped(block, bit):
    devices = range(lax.axis_size("ctx"))
    return lax.ppermute(block, "ctx", [(i, i ^ bit) for i in devices])


def passed_along(block, axis, distance):
    devices = range(lax.axis_size(axis))
    return lax.ppermute(block, axis, [(i - distance, i) for i in devices if i - distance in devices])


def body(queries, keys, values, out_grad, doc_ids):
    q_rows, d_rows = queries[0], out_grad[0]
    place = lax.axis_index("ctx") % GROUP_SHARDS
    odd_core = place % CHIP == 1
    second_chip = place >= CHIP
    own = pack(keys[0], values[0], doc_ids)
    back = passed_along(own, "ctx", REACH)
    other_chip = swapped(jnp.where(second_chip, back, own), CHIP)
    near = swapped(jnp.where(odd_core, back, own), 1)
    across = swapped(other_chip, 1)
    blocks = (own, back, other_chip, near, across)
    acts, dqs, parts = [], [], []
    for first in range(0, HK, HALF):
        attended, grad_q, g_own, g_back, g_chip, g_near, g_across = attend(
            q_rows, d_rows, blocks, first, HALF
        )
        acts.append(passed_along(attended, "pipe", 1))
        dqs.append(passed_along(grad_q, "pipe", -1))
        got = swapped(jnp.concatenate([g_near, g_across], axis=0), 1)
        got_near, got_across = got[:2], got[2:]
        got_chip = swapped(g_chip + got_across, CHIP)
        g_back = g_back + jnp.where(odd_core, got_near, 0.0) + jnp.where(second_chip, got_chip, 0.0)
        g_own = g_own + jnp.where(odd_core, 0.0, got_near) + jnp.where(second_chip, 0.0, got_chip)
        got_back = passed_along(g_back, "ctx", -REACH)
        parts += [g_own, got_back]
    key_grads, value_grads = finish(parts)
    acts_in = jnp.concatenate(acts, axis=1)
    dq_in = jnp.concatenate(dqs, axis=1)
    return acts_in[None], dq_in[None], key_grads[None], value_grads[None]


def solution(mesh):
    wide = P("pipe", "ctx", None)
    in_specs = (wide, wide, wide, wide, P("pipe", "ctx"))
    return jax.shard_map(body, mesh=mesh, in_specs=in_specs, out_specs=(wide,) * 4, check_vma=False)
```

time: 204 us -> 136 us (0.67)
  the two profiles are of different devices: /device:TPU:409 before, /device:TPU:280 now
where the time goes in v1:
time: 136 us; the launch traced here: 135 us
  starting transfers between devices  62.3 us (46%)
  waiting for transfers between devices  44.6 us (33%)
  Pallas kernels  20.5 us (15%)
  other arithmetic  4.82 us (4%)
  local copies, waits for them, and re-layouts  1.94 us (1%)
    ppermute x7, starting transfers between devices, swapped(): return lax.ppermute(block, 'ctx', [(i, i ^ bit) for i in devices])  37.7 us
    ppermute x7, waiting for transfers between devices, passed_along(): lax.ppermute(block, axis, [(i - distance, i) for i in devices if i - dist...  26.5 us
    ppermute x7, starting transfers between devices, passed_along(): lax.ppermute(block, axis, [(i - distance, i) for i in devices if i - dist...  24.6 us
    ppermute x7, waiting for transfers between devices, swapped(): return lax.ppermute(block, 'ctx', [(i, i ^ bit) for i in devices])  18 us
    pallas_call x2, Pallas kernels, attend(): pl.pallas_call(kernel, grid=(count,), in_specs=[wide] * 2 + [k_spec] * 5...  16.7 us
  transfers between devices with their start and end apart: 14, of which 9 were waited for; matrix products, arithmetic and copies ran while one was open for 3% of the time, Pallas kernels for 6%

profile of v1, /device:TPU:280, one launch (start us, length us, event | category | flops | bytes accessed | tf_op | source)
XLA Modules:
  0.0 135.0 jit_solution(4971460929006842068)
XLA Ops:
  0.6 1.8 %shard_map.84.refs_2_.refs_7_.refs_12_ = bf16[1040,128]{1,0:T(8,128)(2,1)} custom-call(bf16[128,512]{1,0:T(8,128)(2,1)} %bitcast.14, bf16[128,512]{1,0:T(8,128)(2,1)} %bitcast.15, s32[1,128]{1,0:T(1,128)} %m_ref.1), custom_call_target="tpu_custom_call" | custom-call | tf_op jit(solution)/shard_map/pallas_call | solution.py:162
  2.5 4.8 %collective-permute-start = (bf16[1040,128]{1,0:T(8,128)(2,1)}, bf16[1040,128]{1,0:T(8,128)(2,1)S(1)}, u32[]{:S(2)}, u32[]{:S(2)}) collective-permute-start(bf16[1040,128]{1,0:T(8,128)(2,1)} %shard_map.84.refs_2_.refs_7_.refs_12_), channel_id=1, source_target_pairs={{0,4},{1,5},{2,6},{3,7},{4,8},{5,9},{6,10},{7,11},{8,12},{9,13},{1... | collective-permute-start | bytes 798728 | tf_op jit(solution)/shard_map/ppermute | solution.py:192
  7.3 5.9 %collective-permute-done.refs_3_.refs_8_.refs_13_ = bf16[1040,128]{1,0:T(8,128)(2,1)S(1)} collective-permute-done((bf16[1040,128]{1,0:T(8,128)(2,1)}, bf16[1040,128]{1,0:T(8,128)(2,1)S(1)}, u32[]{:S(2)}, u32[]{:S(2)}) %collective-permute-start) | collective-permute-done | bytes 266272 | tf_op jit(solution)/shard_map/ppermute | solution.py:192
  13.2 1.0 broadcast_select_fusion
  14.2 3.4 %collective-permute-start.1 = (bf16[1040,128]{1,0:T(8,128)(2,1)S(1)}, bf16[1040,128]{1,0:T(8,128)(2,1)S(1)}, u32[]{:S(2)}, u32[]{:S(2)}) collective-permute-start(bf16[1040,128]{1,0:T(8,128)(2,1)S(1)} %get-tuple-element.41), channel_id=1, source_target_pairs={{0,2},{1,3},{2,0},{3,1},{4,6},{5,7},{6,4},{7,5},{8,10},{9,11},{10,... | collective-permute-start | bytes 798728 | tf_op jit(solution)/shard_map/ppermute | solution.py:187
  17.6 1.9 %collective-permute-start.2 = (bf16[1040,128]{1,0:T(8,128)(2,1)S(1)}, bf16[1040,128]{1,0:T(8,128)(2,1)S(1)}, u32[]{:S(2)}, u32[]{:S(2)}) collective-permute-start(bf16[1040,128]{1,0:T(8,128)(2,1)S(1)} %get-tuple-element.40), channel_id=1, source_target_pairs={{0,1},{1,0},{2,3},{3,2},{4,5},{5,4},{6,7},{7,6},{8,9},{9,8},{10,11... | collective-permute-start | bytes 798728 | tf_op jit(solution)/shard_map/ppermute | solution.py:187
  19.5 3.8 %collective-permute-done.1.refs_4_.refs_9_.refs_14_ = bf16[1040,128]{1,0:T(8,128)(2,1)S(1)} collective-permute-done((bf16[1040,128]{1,0:T(8,128)(2,1)S(1)}, bf16[1040,128]{1,0:T(8,128)(2,1)S(1)}, u32[]{:S(2)}, u32[]{:S(2)}) %collective-permute-start.1) | collective-permute-done | bytes 266272 | tf_op jit(solution)/shard_map/ppermute | solution.py:187
  23.4 1.9 %collective-permute-start.3 = (bf16[1040,128]{1,0:T(8,128)(2,1)S(1)}, bf16[1040,128]{1,0:T(8,128)(2,1)S(1)}, u32[]{:S(2)}, u32[]{:S(2)}) collective-permute-start(bf16[1040,128]{1,0:T(8,128)(2,1)S(1)} %collective-permute-done.1.refs_4_.refs_9_.refs_14_), channel_id=1, source_target_pairs={{0,1},{1,0},{2,3},{3,2},{4,5},{5,4},{6,7},{7,6},{8,9},{9,8},{10,11... | collective-permute-start | bytes 798728 | tf_op jit(solution)/shard_map/ppermute | solution.py:187
  25.3 1.5 %collective-permute-done.3.refs_6_.refs_11_.refs_16_ = bf16[1040,128]{1,0:T(8,128)(2,1)S(1)} collective-permute-done((bf16[1040,128]{1,0:T(8,128)(2,1)S(1)}, bf16[1040,128]{1,0:T(8,128)(2,1)S(1)}, u32[]{:S(2)}, u32[]{:S(2)}) %collective-permute-start.3) | collective-permute-done | bytes 266272 | tf_op jit(solution)/shard_map/ppermute | solution.py:187
  26.8 1.2 copy-done.2
  28.0 8.3 %shard_map.86 = (bf16[128,2048]{1,0:T(8,128)(2,1)S(1)}, bf16[128,2048]{1,0:T(8,128)(2,1)S(1)}, f32[2,2,128,128]{3,2,1,0:T(8,128)S(1)}, f32[2,2,128,128]{3,2,1,0:...) custom-call(bf16[128,4096]{1,0:T(8,128)(2,1)S(1)} %bitcast.10, ...), custom_call_target="tpu_custom_call" | custom-call | flops 2013265920 | bytes 8388608 | tf_op jit(solution)/shard_map/pallas_call | solution.py:126
  36.4 2.0 %collective-permute-start.11 = (f32[4,2,128,128]{3,2,1,0:T(8,128)S(1)}, f32[4,2,128,128]{3,2,1,0:T(8,128)S(1)}, u32[]{:S(2)}, u32[]{:S(2)}) collective-permute-start(f32[4,2,128,128]{3,2,1,0:T(8,128)S(1)} %pad_maximum_fusion.1), channel_id=1, source_target_pairs={{0,1},{1,0},{2,3},{3,2},{4,5},{5,4},{6,7},{7,6},{8,9},{9,8},{10,11... | collective-permute-start | bytes 1572872 | tf_op jit(solution)/shard_map/ppermute | solution.py:187
  38.5 8.4 %shard_map.85 = (bf16[128,2048]{1,0:T(8,128)(2,1)S(1)}, bf16[128,2048]{1,0:T(8,128)(2,1)S(1)}, f32[2,2,128,128]{3,2,1,0:T(8,128)S(1)}, f32[2,2,128,128]{3,2,1,0:...) custom-call(bf16[128,4096]{1,0:T(8,128)(2,1)S(1)} %bitcast.11, ...), custom_call_target="tpu_custom_call" | custom-call | flops 2013265920 | bytes 8388608 | tf_op jit(solution)/shard_map/pallas_call | solution.py:126
  46.9 2.3 %collective-permute-start.8 = (f32[4,2,128,128]{3,2,1,0:T(8,128)S(1)}, f32[4,2,128,128]{3,2,1,0:T(8,128)S(1)}, u32[]{:S(2)}, u32[]{:S(2)}) collective-permute-start(f32[4,2,128,128]{3,2,1,0:T(8,128)S(1)} %pad_maximum_fusion), channel_id=1, source_target_pairs={{0,1},{1,0},{2,3},{3,2},{4,5},{5,4},{6,7},{7,6},{8,9},{9,8},{10,11... | collective-permute-start | bytes 1572872 | tf_op jit(solution)/shard_map/ppermute | solution.py:187
  49.2 3.4 %collective-permute-start.5 = (bf16[128,2048]{1,0:T(8,128)(2,1)S(1)}, bf16[128,2048]{1,0:T(8,128)(2,1)S(1)}, u32[]{:S(2)}, u32[]{:S(2)}) collective-permute-start(bf16[128,2048]{1,0:T(8,128)(2,1)S(1)} %get-tuple-element.21), channel_id=1, source_target_pairs={{0,32},{32,64},{64,96},{96,128},{128,160},{160,192},{192,224},{224... | collective-permute-start | bytes 1572872 | tf_op jit(solution)/shard_map/ppermute | solution.py:192
  52.6 3.4 %collective-permute-start.4 = (bf16[128,2048]{1,0:T(8,128)(2,1)S(1)}, bf16[128,2048]{1,0:T(8,128)(2,1)S(1)}, u32[]{:S(2)}, u32[]{:S(2)}) collective-permute-start(bf16[128,2048]{1,0:T(8,128)(2,1)S(1)} %get-tuple-element.20), channel_id=1, source_target_pairs={{0,32},{32,64},{64,96},{96,128},{128,160},{160,192},{192,224},{224... | collective-permute-start | bytes 1572872 | tf_op jit(solution)/shard_map/ppermute | solution.py:192
  56.0 6.7 %collective-permute-start.7 = (bf16[128,2048]{1,0:T(8,128)(2,1)S(1)}, bf16[128,2048]{1,0:T(8,128)(2,1)S(1)}, u32[]{:S(2)}, u32[]{:S(2)}) collective-permute-start(bf16[128,2048]{1,0:T(8,128)(2,1)S(1)} %get-tuple-element.23), channel_id=1, source_target_pairs={{32,0},{64,32},{96,64},{128,96},{160,128},{192,160},{224,192},{256... | collective-permute-start | bytes 1572872 | tf_op jit(solution)/shard_map/ppermute | solution.py:192
  62.7 2.4 %collective-permute-start.6 = (bf16[128,2048]{1,0:T(8,128)(2,1)S(1)}, bf16[128,2048]{1,0:T(8,128)(2,1)S(1)}, u32[]{:S(2)}, u32[]{:S(2)}) collective-permute-start(bf16[128,2048]{1,0:T(8,128)(2,1)S(1)} %get-tuple-element.22), channel_id=1, source_target_pairs={{32,0},{64,32},{96,64},{128,96},{160,128},{192,160},{224,192},{256... | collective-permute-start | bytes 1572872 | tf_op jit(solution)/shard_map/ppermute | solution.py:192
  65.2 3.4 %collective-permute-start.12 = (f32[2,2,128,128]{3,2,1,0:T(8,128)S(1)}, f32[2,2,128,128]{3,2,1,0:T(8,128)S(1)}, u32[]{:S(2)}, u32[]{:S(2)}) collective-permute-start(f32[2,2,128,128]{3,2,1,0:T(8,128)S(1)} %slice_add_fusion), channel_id=1, source_target_pairs={{0,2},{1,3},{2,0},{3,1},{4,6},{5,7},{6,4},{7,5},{8,10},{9,11},{10,... | collective-permute-start | bytes 786440 | tf_op jit(solution)/shard_map/ppermute | solution.py:187
  68.6 1.5 %collective-permute-done.5 = bf16[128,2048]{1,0:T(8,128)(2,1)S(1)} collective-permute-done((bf16[128,2048]{1,0:T(8,128)(2,1)S(1)}, bf16[128,2048]{1,0:T(8,128)(2,1)S(1)}, u32[]{:S(2)}, u32[]{:S(2)}) %collective-permute-start.5) | collective-permute-done | bytes 524320 | tf_op jit(solution)/shard_map/ppermute | solution.py:192
  70.2 22.8 %collective-permute-start.9 = (f32[2,2,128,128]{3,2,1,0:T(8,128)S(1)}, f32[2,2,128,128]{3,2,1,0:T(8,128)S(1)}, u32[]{:S(2)}, u32[]{:S(2)}) collective-permute-start(f32[2,2,128,128]{3,2,1,0:T(8,128)S(1)} %slice_add_fusion.1), channel_id=1, source_target_pairs={{0,2},{1,3},{2,0},{3,1},{4,6},{5,7},{6,4},{7,5},{8,10},{9,11},{10,... | collective-permute-start | bytes 786440 | tf_op jit(solution)/shard_map/ppermute | solution.py:187
  93.0 10.8 %collective-permute-done.4 = bf16[128,2048]{1,0:T(8,128)(2,1)S(1)} collective-permute-done((bf16[128,2048]{1,0:T(8,128)(2,1)S(1)}, bf16[128,2048]{1,0:T(8,128)(2,1)S(1)}, u32[]{:S(2)}, u32[]{:S(2)}) %collective-permute-start.4) | collective-permute-done | bytes 524320 | tf_op jit(solution)/shard_map/ppermute | solution.py:192
  103.7 1.1 maximum_bitcast_fusion
  104.8 10.5 %collective-permute-done.12 = f32[2,2,128,128]{3,2,1,0:T(8,128)S(1)} collective-permute-done((f32[2,2,128,128]{3,2,1,0:T(8,128)S(1)}, f32[2,2,128,128]{3,2,1,0:T(8,128)S(1)}, u32[]{:S(2)}, u32[]{:S(2)}) %collective-permute-start.12) | collective-permute-done | bytes 262176 | tf_op jit(solution)/shard_map/ppermute | solution.py:187
  116.1 1.9 %collective-permute-start.13 = (f32[2,2,128,128]{3,2,1,0:T(8,128)S(1)}, f32[2,2,128,128]{3,2,1,0:T(8,128)S(1)}, u32[]{:S(2)}, u32[]{:S(2)}) collective-permute-start(f32[2,2,128,128]{3,2,1,0:T(8,128)S(1)} %get-tuple-element.36), channel_id=1, source_target_pairs={{4,0},{5,1},{6,2},{7,3},{8,4},{9,5},{10,6},{11,7},{12,8},{13,9},{1... | collective-permute-start | bytes 786440 | tf_op jit(solution)/shard_map/ppermute | solution.py:192
  118.0 2.2 %collective-permute-done.9 = f32[2,2,128,128]{3,2,1,0:T(8,128)S(1)} collective-permute-done((f32[2,2,128,128]{3,2,1,0:T(8,128)S(1)}, f32[2,2,128,128]{3,2,1,0:T(8,128)S(1)}, u32[]{:S(2)}, u32[]{:S(2)}) %collective-permute-start.9) | collective-permute-done | bytes 262176 | tf_op jit(solution)/shard_map/ppermute | solution.py:187
  120.2 0.8 select_add_fusion.2
  121.0 1.9 %collective-permute-start.10 = (f32[2,2,128,128]{3,2,1,0:T(8,128)S(1)}, f32[2,2,128,128]{3,2,1,0:T(8,128)S(1)}, u32[]{:S(2)}, u32[]{:S(2)}) collective-permute-start(f32[2,2,128,128]{3,2,1,0:T(8,128)S(1)} %get-tuple-element.38), channel_id=1, source_target_pairs={{4,0},{5,1},{6,2},{7,3},{8,4},{9,5},{10,6},{11,7},{12,8},{13,9},{1... | collective-permute-start | bytes 786440 | tf_op jit(solution)/shard_map/ppermute | solution.py:192
  122.9 1.1 maximum_bitcast_fusion.1
  124.0 2.7 %collective-permute-done.13.refs_3_ = f32[2,2,128,128]{3,2,1,0:T(8,128)S(1)} collective-permute-done((f32[2,2,128,128]{3,2,1,0:T(8,128)S(1)}, f32[2,2,128,128]{3,2,1,0:T(8,128)S(1)}, u32[]{:S(2)}, u32[]{:S(2)}) %collective-permute-start.13) | collective-permute-done | bytes 262176 | tf_op jit(solution)/shard_map/ppermute | solution.py:192
  126.7 5.6 %collective-permute-done.10.refs_1_ = f32[2,2,128,128]{3,2,1,0:T(8,128)S(1)} collective-permute-done((f32[2,2,128,128]{3,2,1,0:T(8,128)S(1)}, f32[2,2,128,128]{3,2,1,0:T(8,128)S(1)}, u32[]{:S(2)}, u32[]{:S(2)}) %collective-permute-start.10) | collective-permute-done | bytes 262176 | tf_op jit(solution)/shard_map/ppermute | solution.py:192
  133.0 1.9 %shard_map.87 = (bf16[128,512]{1,0:T(8,128)(2,1)}, bf16[128,512]{1,0:T(8,128)(2,1)}) custom-call(f32[2,2,128,128]{3,2,1,0:T(8,128)} %get-tuple-element.39.refs_0_, f32[2,2,128,128]{3,2,1,0:T(8,128)} %copy-done.4, f32[2,2,128,128]{3,2,1,0:T(8,128)} %get-tuple-element.37.refs_2_, f32[2,2,128,128]{3,2,1,0:T(8,128)} %copy-done.3), custom_call_target="tpu_custom_call" | custom-call | tf_op jit(solution)/shard_map/pallas_call | solution.py:179
  (19 shorter events, 1.7 us)
Async XLA Ops:
  0.6 26.2 %copy-start.1 = (bf16[1,128,4096]{2,1,0:T(8,128)(2,1)S(1)}, bf16[1,128,4096]{2,1,0:T(8,128)(2,1)}, u32[]{:S(2)}) copy-start(bf16[1,128,4096]{2,1,0:T(8,128)(2,1)} %param.5) | copy-start | bytes 3145732
  2.5 24.3 %copy-start = (bf16[1040,128]{1,0:T(8,128)(2,1)S(1)}, bf16[1040,128]{1,0:T(8,128)(2,1)}, u32[]{:S(2)}) copy-start(bf16[1040,128]{1,0:T(8,128)(2,1)} %shard_map.84.refs_2_.refs_7_.refs_12_) | copy-start | bytes 798724
  2.5 10.8 %collective-permute-start = (bf16[1040,128]{1,0:T(8,128)(2,1)}, bf16[1040,128]{1,0:T(8,128)(2,1)S(1)}, u32[]{:S(2)}, u32[]{:S(2)}) collective-permute-start(bf16[1040,128]{1,0:T(8,128)(2,1)} %shard_map.84.refs_2_.refs_7_.refs_12_), channel_id=1, source_target_pairs={{0,4},{1,5},{2,6},{3,7},{4,8},{5,9},{6,10},{7,11},{8,12},{9,13},{1... | collective-permute-start | bytes 798728 | tf_op jit(solution)/shard_map/ppermute | solution.py:192
  14.2 9.2 %collective-permute-start.1 = (bf16[1040,128]{1,0:T(8,128)(2,1)S(1)}, bf16[1040,128]{1,0:T(8,128)(2,1)S(1)}, u32[]{:S(2)}, u32[]{:S(2)}) collective-permute-start(bf16[1040,128]{1,0:T(8,128)(2,1)S(1)} %get-tuple-element.41), channel_id=1, source_target_pairs={{0,2},{1,3},{2,0},{3,1},{4,6},{5,7},{6,4},{7,5},{8,10},{9,11},{10,... | collective-permute-start | bytes 798728 | tf_op jit(solution)/shard_map/ppermute | solution.py:187
  17.6 7.7 %collective-permute-start.2 = (bf16[1040,128]{1,0:T(8,128)(2,1)S(1)}, bf16[1040,128]{1,0:T(8,128)(2,1)S(1)}, u32[]{:S(2)}, u32[]{:S(2)}) collective-permute-start(bf16[1040,128]{1,0:T(8,128)(2,1)S(1)} %get-tuple-element.40), channel_id=1, source_target_pairs={{0,1},{1,0},{2,3},{3,2},{4,5},{5,4},{6,7},{7,6},{8,9},{9,8},{10,11... | collective-permute-start | bytes 798728 | tf_op jit(solution)/shard_map/ppermute | solution.py:187
  23.4 3.4 %collective-permute-start.3 = (bf16[1040,128]{1,0:T(8,128)(2,1)S(1)}, bf16[1040,128]{1,0:T(8,128)(2,1)S(1)}, u32[]{:S(2)}, u32[]{:S(2)}) collective-permute-start(bf16[1040,128]{1,0:T(8,128)(2,1)S(1)} %collective-permute-done.1.refs_4_.refs_9_.refs_14_), channel_id=1, source_target_pairs={{0,1},{1,0},{2,3},{3,2},{4,5},{5,4},{6,7},{7,6},{8,9},{9,8},{10,11... | collective-permute-start | bytes 798728 | tf_op jit(solution)/shard_map/ppermute | solution.py:187
  26.8 1.2 copy-start.2
  36.4 26.2 %collective-permute-start.11 = (f32[4,2,128,128]{3,2,1,0:T(8,128)S(1)}, f32[4,2,128,128]{3,2,1,0:T(8,128)S(1)}, u32[]{:S(2)}, u32[]{:S(2)}) collective-permute-start(f32[4,2,128,128]{3,2,1,0:T(8,128)S(1)} %pad_maximum_fusion.1), channel_id=1, source_target_pairs={{0,1},{1,0},{2,3},{3,2},{4,5},{5,4},{6,7},{7,6},{8,9},{9,8},{10,11... | collective-permute-start | bytes 1572872 | tf_op jit(solution)/shard_map/ppermute | solution.py:187
  46.9 18.3 %collective-permute-start.8 = (f32[4,2,128,128]{3,2,1,0:T(8,128)S(1)}, f32[4,2,128,128]{3,2,1,0:T(8,128)S(1)}, u32[]{:S(2)}, u32[]{:S(2)}) collective-permute-start(f32[4,2,128,128]{3,2,1,0:T(8,128)S(1)} %pad_maximum_fusion), channel_id=1, source_target_pairs={{0,1},{1,0},{2,3},{3,2},{4,5},{5,4},{6,7},{7,6},{8,9},{9,8},{10,11... | collective-permute-start | bytes 1572872 | tf_op jit(solution)/shard_map/ppermute | solution.py:187
  49.2 21.0 %collective-permute-start.5 = (bf16[128,2048]{1,0:T(8,128)(2,1)S(1)}, bf16[128,2048]{1,0:T(8,128)(2,1)S(1)}, u32[]{:S(2)}, u32[]{:S(2)}) collective-permute-start(bf16[128,2048]{1,0:T(8,128)(2,1)S(1)} %get-tuple-element.21), channel_id=1, source_target_pairs={{0,32},{32,64},{64,96},{96,128},{128,160},{160,192},{192,224},{224... | collective-permute-start | bytes 1572872 | tf_op jit(solution)/shard_map/ppermute | solution.py:192
  52.6 51.1 %collective-permute-start.4 = (bf16[128,2048]{1,0:T(8,128)(2,1)S(1)}, bf16[128,2048]{1,0:T(8,128)(2,1)S(1)}, u32[]{:S(2)}, u32[]{:S(2)}) collective-permute-start(bf16[128,2048]{1,0:T(8,128)(2,1)S(1)} %get-tuple-element.20), channel_id=1, source_target_pairs={{0,32},{32,64},{64,96},{96,128},{128,160},{160,192},{192,224},{224... | collective-permute-start | bytes 1572872 | tf_op jit(solution)/shard_map/ppermute | solution.py:192
  56.0 66.9 %collective-permute-start.7 = (bf16[128,2048]{1,0:T(8,128)(2,1)S(1)}, bf16[128,2048]{1,0:T(8,128)(2,1)S(1)}, u32[]{:S(2)}, u32[]{:S(2)}) collective-permute-start(bf16[128,2048]{1,0:T(8,128)(2,1)S(1)} %get-tuple-element.23), channel_id=1, source_target_pairs={{32,0},{64,32},{96,64},{128,96},{160,128},{192,160},{224,192},{256... | collective-permute-start | bytes 1572872 | tf_op jit(solution)/shard_map/ppermute | solution.py:192
  62.7 60.3 %collective-permute-start.6 = (bf16[128,2048]{1,0:T(8,128)(2,1)S(1)}, bf16[128,2048]{1,0:T(8,128)(2,1)S(1)}, u32[]{:S(2)}, u32[]{:S(2)}) collective-permute-start(bf16[128,2048]{1,0:T(8,128)(2,1)S(1)} %get-tuple-element.22), channel_id=1, source_target_pairs={{32,0},{64,32},{96,64},{128,96},{160,128},{192,160},{224,192},{256... | collective-permute-start | bytes 1572872 | tf_op jit(solution)/shard_map/ppermute | solution.py:192
  65.2 50.1 %collective-permute-start.12 = (f32[2,2,128,128]{3,2,1,0:T(8,128)S(1)}, f32[2,2,128,128]{3,2,1,0:T(8,128)S(1)}, u32[]{:S(2)}, u32[]{:S(2)}) collective-permute-start(f32[2,2,128,128]{3,2,1,0:T(8,128)S(1)} %slice_add_fusion), channel_id=1, source_target_pairs={{0,2},{1,3},{2,0},{3,1},{4,6},{5,7},{6,4},{7,5},{8,10},{9,11},{10,... | collective-permute-start | bytes 786440 | tf_op jit(solution)/shard_map/ppermute | solution.py:187
  70.2 50.0 %collective-permute-start.9 = (f32[2,2,128,128]{3,2,1,0:T(8,128)S(1)}, f32[2,2,128,128]{3,2,1,0:T(8,128)S(1)}, u32[]{:S(2)}, u32[]{:S(2)}) collective-permute-start(f32[2,2,128,128]{3,2,1,0:T(8,128)S(1)} %slice_add_fusion.1), channel_id=1, source_target_pairs={{0,2},{1,3},{2,0},{3,1},{4,6},{5,7},{6,4},{7,5},{8,10},{9,11},{10,... | collective-permute-start | bytes 786440 | tf_op jit(solution)/shard_map/ppermute | solution.py:187
  116.1 10.6 %collective-permute-start.13 = (f32[2,2,128,128]{3,2,1,0:T(8,128)S(1)}, f32[2,2,128,128]{3,2,1,0:T(8,128)S(1)}, u32[]{:S(2)}, u32[]{:S(2)}) collective-permute-start(f32[2,2,128,128]{3,2,1,0:T(8,128)S(1)} %get-tuple-element.36), channel_id=1, source_target_pairs={{4,0},{5,1},{6,2},{7,3},{8,4},{9,5},{10,6},{11,7},{12,8},{13,9},{1... | collective-permute-start | bytes 786440 | tf_op jit(solution)/shard_map/ppermute | solution.py:192
  121.0 11.3 %collective-permute-start.10 = (f32[2,2,128,128]{3,2,1,0:T(8,128)S(1)}, f32[2,2,128,128]{3,2,1,0:T(8,128)S(1)}, u32[]{:S(2)}, u32[]{:S(2)}) collective-permute-start(f32[2,2,128,128]{3,2,1,0:T(8,128)S(1)} %get-tuple-element.38), channel_id=1, source_target_pairs={{4,0},{5,1},{6,2},{7,3},{8,4},{9,5},{10,6},{11,7},{12,8},{13,9},{1... | collective-permute-start | bytes 786440 | tf_op jit(solution)/shard_map/ppermute | solution.py:192
  126.7 5.6 %copy-start.3 = (f32[2,2,128,128]{3,2,1,0:T(8,128)}, f32[2,2,128,128]{3,2,1,0:T(8,128)S(1)}, u32[]{:S(2)}) copy-start(f32[2,2,128,128]{3,2,1,0:T(8,128)S(1)} %collective-permute-done.13.refs_3_) | copy-start | bytes 786436
  132.3 0.7 copy-start.4

commit v2 on v1

v2 whole, which is shorter than its diff:
```python
import jax
import jax.numpy as jnp
from jax import lax
from jax.experimental import pallas as pl
from jax.experimental.pallas import tpu as pltpu
from jax.sharding import PartitionSpec as P

HK = 4
DH = 128
GROUP = 8
ROWS = 128
PAIR = 8
MARK_ROWS = 16
SCALING = DH ** (-0.5)
TOP_POWER = 14
LOG2E = 1.4426950408889634
F32 = jnp.float32
BF16 = jnp.bfloat16
NT = (((1,), (1,)), ((), ()))
NN = (((1,), (0,)), ((), ()))


def dot(a, b, dims=NN):
    return lax.dot_general(a, b, dims, preferred_element_type=F32)


def kernel(*refs):
    place, q_ref, d_ref = refs[:3]
    k_refs, v_refs, m_refs = refs[3:9], refs[9:15], refs[15:21]
    attn_ref, dq_ref, turn_ref = refs[21:24]
    own_ref, back_ref, chip_ref, sent_ref = refs[24:28]
    bias, s_sc, p_sc, ds_sc = refs[28:32]
    odd_core = place[0] == 1
    turns_attn = place[1] == 1

    def read(block_refs):
        own, back, chip, across, near_own, near_back = [r[...] for r in block_refs]
        return [own, back, chip, across, jnp.where(odd_core, near_own, near_back)]

    u_pos = lax.broadcasted_iota(jnp.int32, (ROWS, ROWS), 0)
    t_pos = lax.broadcasted_iota(jnp.int32, (ROWS, ROWS), 1)
    tri = u_pos <= t_pos

    @pl.when(pl.program_id(0) == 0)
    def _():
        def col(marks):
            return jnp.transpose(jnp.broadcast_to(marks[0:1, :].astype(F32), (ROWS, ROWS)))

        rows = read(m_refs)
        q_mark = jnp.broadcast_to(rows[0][0:1, :].astype(F32), (ROWS, ROWS))
        marks = [jnp.where(tri, col(rows[0]), col(rows[1]))] + [col(m) for m in rows[2:]]
        for j, k_mark in enumerate(marks):
            bias[j] = jnp.where(k_mark == q_mark, 0.0, -1e30)

    ks = read(k_refs)
    vs = read(v_refs)
    k_t = jnp.concatenate([jnp.transpose(k) for k in ks], axis=1)
    v_t = jnp.concatenate([jnp.transpose(v) for v in vs], axis=1)
    width = PAIR * ROWS
    tri_w = jnp.concatenate([tri] * PAIR, axis=1)
    zero = jnp.zeros((ROWS, width), BF16)

    def merged(blocks):
        return [jnp.where(tri_w, blocks[0], blocks[1])] + list(blocks[2:])

    for unit in range(GROUP // PAIR):
        heads = range(unit * PAIR, (unit + 1) * PAIR)
        cols = slice(unit * width, (unit + 1) * width)
        q_u = jnp.concatenate([q_ref[:, h * DH : (h + 1) * DH] for h in heads], axis=0)
        d_u = jnp.concatenate([d_ref[:, h * DH : (h + 1) * DH] for h in heads], axis=0)
        d_t = jnp.concatenate(
            [jnp.transpose(d_ref[:, h * DH : (h + 1) * DH]) for h in heads], axis=1
        )
        scores = merged([dot(k, q_u, NT) for k in ks])
        top = None
        for j, s in enumerate(scores):
            b = bias[j]
            s = s + jnp.concatenate([b] * PAIR, axis=1)
            s_sc[unit, j] = s
            m = jnp.max(s.reshape(ROWS // 8, 8, width), axis=0)
            top = m if top is None else jnp.maximum(top, m)
        top = jnp.max(top, axis=0, keepdims=True)
        total = None
        for j in range(4):
            e = jnp.exp2((s_sc[unit, j] - top) * (SCALING * LOG2E))
            s_sc[unit, j] = e
            part = jnp.sum(e.reshape(ROWS // 8, 8, width), axis=0)
            total = part if total is None else total + part
        inv = 1.0 / jnp.sum(total, axis=0, keepdims=True)
        for j in range(4):
            w = s_sc[unit, j] * inv
            wb = w.astype(BF16)
            if j == 0:
                p_sc[0, :, cols] = jnp.where(tri_w, wb, zero)
                p_sc[1, :, cols] = jnp.where(tri_w, zero, wb)
            else:
                p_sc[j + 1, :, cols] = wb
        p_all = p_sc[:, :, cols].reshape(5 * ROWS, width)
        att = dot(v_t, p_all).astype(BF16)
        delta = jnp.sum(d_t.astype(F32) * att.astype(F32), axis=0, keepdims=True)
        for i, h in enumerate(heads):
            attn_h = jnp.transpose(att[:, i * ROWS : (i + 1) * ROWS])
            attn_ref[:, h * DH : (h + 1) * DH] = attn_h
            turn_ref[:, h * DH : (h + 1) * DH] = attn_h
        grads = merged([dot(v, d_u, NT) for v in vs])
        for j, gw in enumerate(grads):
            ds = (s_sc[unit, j] * inv * (gw - delta)).astype(BF16)
            if j == 0:
                ds_sc[0, :, cols] = jnp.where(tri_w, ds, zero)
                ds_sc[1, :, cols] = jnp.where(tri_w, zero, ds)
            else:
                ds_sc[j + 1, :, cols] = ds
        ds_all = ds_sc[:, :, cols].reshape(5 * ROWS, width)
        dq = (dot(k_t, ds_all) * SCALING).astype(BF16)
        for i, h in enumerate(heads):
            head = slice(h * DH, (h + 1) * DH)
            dq_h = jnp.transpose(dq[:, i * ROWS : (i + 1) * ROWS])
            dq_ref[:, head] = dq_h
            turn_ref[:, head] = jnp.where(turns_attn, turn_ref[:, head], dq_h)
    q_stack = jnp.concatenate([q_ref[:, h * DH : (h + 1) * DH] for h in range(GROUP)], axis=0)
    d_stack = jnp.concatenate([d_ref[:, h * DH : (h + 1) * DH] for h in range(GROUP)], axis=0)
    dk = dot(ds_sc[...].reshape(5 * ROWS, GROUP * ROWS), q_stack) * SCALING
    dv = dot(p_sc[...].reshape(5 * ROWS, GROUP * ROWS), d_stack)
    def blocks_of(grads):
        return [grads[j * ROWS : (j + 1) * ROWS] for j in range(5)]

    for which, grads in enumerate((dk, dv)):
        own, back, chip, across, near = blocks_of(grads)
        own_ref[which, 0] = own
        peak = jnp.max(jnp.max(jnp.abs(grads[ROWS:]), axis=0, keepdims=True), axis=1, keepdims=True)
        power = jnp.ceil(jnp.log2(jnp.maximum(peak, 1e-30))) - TOP_POWER
        scale = jnp.exp2(-power)
        back_ref[which, 0] = back * scale
        chip_ref[which, 0] = chip * scale
        sent_ref[which, 0] = near * scale
        sent_ref[2 + which, 0] = across * scale
        sent_ref[4 + which, 0] = jnp.broadcast_to(power, (ROWS, DH))


def attend(place, q_rows, d_rows, blocks, first, count, weight):
    width = GROUP * DH
    wide = pl.BlockSpec((ROWS, width), lambda a: (0, first + a))
    wide_out = pl.BlockSpec((ROWS, width), lambda a: (0, a))
    k_spec = pl.BlockSpec((ROWS, DH), lambda a: (first + a, 0))
    v_spec = pl.BlockSpec((ROWS, DH), lambda a: (HK + first + a, 0))
    m_spec = pl.BlockSpec((MARK_ROWS, DH), lambda a: (2 * HK * ROWS // MARK_ROWS, 0))
    g_spec = pl.BlockSpec((2, 1, ROWS, DH), lambda a: (0, a, 0, 0))
    sent_spec = pl.BlockSpec((6, 1, ROWS, DH), lambda a: (0, a, 0, 0))
    pairs = ROWS * ROWS * 5 * GROUP * count
    return pl.pallas_call(
        kernel,
        grid=(count,),
        in_specs=[pl.BlockSpec(memory_space=pltpu.SMEM)] + [wide] * 2 + [k_spec] * 6 + [v_spec] * 6 + [m_spec] * 6,
        out_specs=[wide_out] * 3 + [g_spec] * 3 + [sent_spec],
        out_shape=[jax.ShapeDtypeStruct((ROWS, count * width), BF16)] * 3
        + [jax.ShapeDtypeStruct((2, count, ROWS, DH), F32)] * 3
        + [jax.ShapeDtypeStruct((6, count, ROWS, DH), F32)],
        scratch_shapes=[
            pltpu.VMEM((4, ROWS, ROWS), F32),
            pltpu.VMEM((GROUP // PAIR, 4, ROWS, PAIR * ROWS), F32),
            pltpu.VMEM((5, ROWS, width), BF16),
            pltpu.VMEM((5, ROWS, width), BF16),
        ],
        compiler_params=pltpu.CompilerParams(vmem_limit_bytes=60 * 1024 * 1024),
        cost_estimate=pl.CostEstimate(
            flops=weight * 12 * DH * pairs, bytes_accessed=8 << 20, transcendentals=pairs
        ),
    )(place, q_rows, d_rows, *blocks, *blocks, *blocks)


REACH = 4
CHIP = 2
GROUP_SHARDS = 4
HALF = 4
RUN = 4
SENT = jnp.float16
WEIGHT = 20


def pack_kernel(k_ref, v_ref, m_ref, out_ref):
    for a in range(HK):
        cols = slice(a * DH, (a + 1) * DH)
        out_ref[a * ROWS : (a + 1) * ROWS, :] = k_ref[:, cols]
        out_ref[(HK + a) * ROWS : (HK + a + 1) * ROWS, :] = v_ref[:, cols]
    marks = (m_ref[...] + 1).astype(F32).astype(BF16)
    out_ref[2 * HK * ROWS :, :] = jnp.broadcast_to(marks, (MARK_ROWS, ROWS))


def pack(k_rows, v_rows, marks):
    return pl.pallas_call(
        pack_kernel,
        out_shape=jax.ShapeDtypeStruct((2 * HK * ROWS + MARK_ROWS, DH), BF16),
    )(k_rows, v_rows, marks)


def laid(power):
    rows = power[:, :, 0, :].reshape(2 * HK, DH)
    return jnp.pad(rows, ((0, MARK_ROWS - 2 * HK), (0, 0)))


def parcel(values, power):
    return jnp.concatenate([values.reshape(2 * HK * ROWS, DH), laid(power)], axis=0).astype(SENT)


def swapped(block, bit):
    devices = range(lax.axis_size("ctx"))
    return lax.ppermute(block, "ctx", [(i, i ^ bit) for i in devices])


def passed_along(block, axis, distance):
    devices = range(lax.axis_size(axis))
    return lax.ppermute(block, axis, [(i - distance, i) for i in devices if i - distance in devices])


def relays(shard):
    return shard % CHIP == 1


def over_all(block, step):
    sections, shards = lax.axis_size("pipe"), lax.axis_size("ctx")
    route = []
    for s in range(sections):
        to = s + step
        for c in range(shards):
            if 0 <= to < sections and (to // RUN == s // RUN or not relays(c)):
                route.append((s * shards + c, to * shards + c))
    return lax.ppermute(block, ("pipe", "ctx"), route)


def relay(block, legs):
    shards = lax.axis_size("ctx")
    route = [(s * shards + c, t * shards + c) for s, t in legs for c in range(shards) if relays(c)]
    return lax.ppermute(block, ("pipe", "ctx"), route)


def legs_round(sections):
    runs = range(0, sections, RUN)
    last = RUN - 1
    return [(r + last, r) for r in runs[:-1]] + [(r, r + last) for r in runs[1:]]


def legs_over(sections):
    runs = range(0, sections, RUN)
    last = RUN - 1
    return [(r, r + RUN) for r in runs[:-1]] + [(r + last, r + last - RUN) for r in runs[1:]]


def finish_kernel(own_ref, back_ref, chip_ref, k_ref, v_ref):
    size = 2 * HK * ROWS
    for tile in range(2 * HK):
        which, a = tile // HK, tile % HK
        rows = slice(tile * ROWS, (tile + 1) * ROWS)
        total = own_ref[which, a]
        for ref in (back_ref, chip_ref):
            total = total + ref[rows] * jnp.exp2(ref[size + tile : size + tile + 1, :])
        out = (k_ref, v_ref)[which]
        out[:, a * DH : (a + 1) * DH] = total.astype(BF16)


def finish(*parts):
    return pl.pallas_call(
        finish_kernel,
        out_shape=[jax.ShapeDtypeStruct((ROWS, HK * DH), BF16)] * 2,
    )(*parts)


def body(queries, keys, values, out_grad, doc_ids):
    q_rows, d_rows = queries[0], out_grad[0]
    place = lax.axis_index("ctx") % GROUP_SHARDS
    odd_core = place % CHIP == 1
    second_chip = place >= CHIP
    turn = lax.axis_index("pipe") % RUN
    first_in_run, last_in_run = turn == 0, turn == RUN - 1
    own = pack(keys[0], values[0], doc_ids)
    chip = passed_along(own, "ctx", CHIP)
    back = passed_along(own, "ctx", REACH)
    near_own = swapped(own, 1)
    near_back = swapped(back, 1)
    across = swapped(chip, 1)
    blocks = (own, back, chip, across, near_own, near_back)
    flags = jnp.stack([odd_core, last_in_run]).astype(jnp.int32)
    attended, grad_q, turned, g_own, g_back, g_chip, sent = attend(
        flags, q_rows, d_rows, blocks, 0, HK, WEIGHT
    )
    sections = lax.axis_size("pipe")
    turned = relay(turned, legs_round(sections))
    acts_in = over_all(attended, 1)
    dq_in = over_all(grad_q, -1)
    got = swapped(sent.astype(SENT), 1)
    turned, got = lax.optimization_barrier((turned, got))
    power, got_power = sent[4:], got[4:].astype(F32)
    got_near, got_across = got[:2].astype(F32), got[2:4].astype(F32)
    both = jnp.maximum(power, got_power) + 1
    mine = jnp.exp2(power - both)
    theirs = jnp.exp2(got_power - both)
    theirs_back = jnp.where(odd_core, theirs, 0.0)
    theirs_own = jnp.where(odd_core, 0.0, jnp.exp2(got_power))
    for_chip = parcel(g_chip * mine + got_across * theirs, both)
    for_back = parcel(g_back * mine + got_near * theirs_back, both)
    got_chip = passed_along(for_chip, "ctx", -CHIP)
    got_back = passed_along(for_back, "ctx", -REACH)
    turned = relay(turned, legs_over(sections))
    g_own = g_own + got_near * theirs_own
    key_grads, value_grads = finish(g_own, got_back.astype(F32), got_chip.astype(F32))
    acts_in = jnp.where(odd_core & first_in_run, turned, acts_in)
    dq_in = jnp.where(odd_core & last_in_run, turned, dq_in)
    return acts_in[None], dq_in[None], key_grads[None], value_grads[None]


def solution(mesh):
    wide = P("pipe", "ctx", None)
    in_specs = (wide, wide, wide, wide, P("pipe", "ctx"))
    return jax.shard_map(body, mesh=mesh, in_specs=in_specs, out_specs=(wide,) * 4, check_vma=False)
```

time: 136 us -> 94.6 us (0.70)
  the two profiles are of different devices: /device:TPU:280 before, /device:TPU:167 now
where the time goes in v2:
time: 94.6 us; the launch traced here: 94 us
  waiting for transfers between devices  33.8 us (36%)
  starting transfers between devices  31.9 us (34%)
  Pallas kernels  17.9 us (19%)
  other arithmetic  8.75 us (9%)
    ppermute x4, waiting for transfers between devices, passed_along(): lax.ppermute(block, axis, [(i - distance, i) for i in devices if i - dist...  21.3 us
    pallas_call x1, Pallas kernels, attend(): pl.pallas_call(kernel, grid=(count,), in_specs=[pl.BlockSpec(memory_space...  14 us
    ppermute x4, starting transfers between devices, swapped(): return lax.ppermute(block, 'ctx', [(i, i ^ bit) for i in devices])  11.7 us
    ppermute x2, waiting for transfers between devices, relay(): return lax.ppermute(block, ('pipe', 'ctx'), route)  11.6 us
    ppermute x4, starting transfers between devices, passed_along(): lax.ppermute(block, axis, [(i - distance, i) for i in devices if i - dist...  10.7 us
    ppermute x2, starting transfers between devices, over_all(): return lax.ppermute(block, ('pipe', 'ctx'), route)  5.34 us
    ppermute x2, starting transfers between devices, relay(): return lax.ppermute(block, ('pipe', 'ctx'), route)  4.15 us
    pallas_call x1, Pallas kernels, finish(): pl.pallas_call(finish_kernel, out_shape=[jax.ShapeDtypeStruct((ROWS, HK *...  2.12 us
  transfers between devices with their start and end apart: 12, of which 4 were waited for; matrix products, arithmetic and copies ran while one was open for 8% of the time, Pallas kernels for 2%

profile of v2, /device:TPU:167, one launch (start us, length us, event | category | flops | bytes accessed | tf_op | source)
XLA Modules:
  0.0 94.0 jit_solution(2424005254059585219)
XLA Ops:
  0.6 1.7 %shard_map.84.refs_3_.refs_9_.refs_15_ = bf16[1040,128]{1,0:T(8,128)(2,1)} custom-call(bf16[128,512]{1,0:T(8,128)(2,1)} %bitcast.17, bf16[128,512]{1,0:T(8,128)(2,1)} %bitcast.18, s32[1,128]{1,0:T(1,128)} %m_ref.1), custom_call_target="tpu_custom_call" | custom-call | tf_op jit(solution)/shard_map/pallas_call | solution.py:190
  2.4 4.0 %collective-permute-start.1 = (bf16[1040,128]{1,0:T(8,128)(2,1)}, bf16[1040,128]{1,0:T(8,128)(2,1)S(1)}, u32[]{:S(2)}, u32[]{:S(2)}) collective-permute-start(bf16[1040,128]{1,0:T(8,128)(2,1)} %shard_map.84.refs_3_.refs_9_.refs_15_), channel_id=1, source_target_pairs={{0,2},{1,3},{2,4},{3,5},{4,6},{5,7},{6,8},{7,9},{8,10},{9,11},{10,... | collective-permute-start | bytes 798728 | tf_op jit(solution)/shard_map/ppermute | solution.py:212
  6.4 2.3 %collective-permute-start = (bf16[1040,128]{1,0:T(8,128)(2,1)}, bf16[1040,128]{1,0:T(8,128)(2,1)S(1)}, u32[]{:S(2)}, u32[]{:S(2)}) collective-permute-start(bf16[1040,128]{1,0:T(8,128)(2,1)} %shard_map.84.refs_3_.refs_9_.refs_15_), channel_id=1, source_target_pairs={{0,4},{1,5},{2,6},{3,7},{4,8},{5,9},{6,10},{7,11},{8,12},{9,13},{1... | collective-permute-start | bytes 798728 | tf_op jit(solution)/shard_map/ppermute | solution.py:212
  8.7 3.1 %collective-permute-start.3 = (bf16[1040,128]{1,0:T(8,128)(2,1)}, bf16[1040,128]{1,0:T(8,128)(2,1)S(1)}, u32[]{:S(2)}, u32[]{:S(2)}) collective-permute-start(bf16[1040,128]{1,0:T(8,128)(2,1)} %shard_map.84.refs_3_.refs_9_.refs_15_), channel_id=1, source_target_pairs={{0,1},{1,0},{2,3},{3,2},{4,5},{5,4},{6,7},{7,6},{8,9},{9,8},{10,11... | collective-permute-start | bytes 798728 | tf_op jit(solution)/shard_map/ppermute | solution.py:207
  11.8 2.0 %collective-permute-done.1.refs_5_.refs_11_.refs_17_ = bf16[1040,128]{1,0:T(8,128)(2,1)S(1)} collective-permute-done((bf16[1040,128]{1,0:T(8,128)(2,1)}, bf16[1040,128]{1,0:T(8,128)(2,1)S(1)}, u32[]{:S(2)}, u32[]{:S(2)}) %collective-permute-start.1) | collective-permute-done | bytes 266272 | tf_op jit(solution)/shard_map/ppermute | solution.py:212
  13.8 4.6 %collective-permute-start.2 = (bf16[1040,128]{1,0:T(8,128)(2,1)S(1)}, bf16[1040,128]{1,0:T(8,128)(2,1)S(1)}, u32[]{:S(2)}, u32[]{:S(2)}) collective-permute-start(bf16[1040,128]{1,0:T(8,128)(2,1)S(1)} %collective-permute-done.1.refs_5_.refs_11_.refs_17_), channel_id=1, source_target_pairs={{0,1},{1,0},{2,3},{3,2},{4,5},{5,4},{6,7},{7,6},{8,9},{9,8},{10,11... | collective-permute-start | bytes 798728 | tf_op jit(solution)/shard_map/ppermute | solution.py:207
  18.4 0.0 collective-permute-done.refs_4_.refs_10_.refs_16_
  18.5 1.9 %collective-permute-start.4 = (bf16[1040,128]{1,0:T(8,128)(2,1)S(1)}, bf16[1040,128]{1,0:T(8,128)(2,1)S(1)}, u32[]{:S(2)}, u32[]{:S(2)}) collective-permute-start(bf16[1040,128]{1,0:T(8,128)(2,1)S(1)} %collective-permute-done.refs_4_.refs_10_.refs_16_), channel_id=1, source_target_pairs={{0,1},{1,0},{2,3},{3,2},{4,5},{5,4},{6,7},{7,6},{8,9},{9,8},{10,11... | collective-permute-start | bytes 798728 | tf_op jit(solution)/shard_map/ppermute | solution.py:207
  20.4 0.6 add_convert_fusion.1.refs_0_
  21.0 0.0 collective-permute-done.3.refs_7_.refs_13_.refs_19_
  21.0 0.0 collective-permute-done.2.refs_6_.refs_12_.refs_18_
  21.0 0.9 collective-permute-done.4.refs_8_.refs_14_.refs_20_
  21.9 0.7 copy-done.8
  22.6 14.0 %shard_map.85 = (bf16[128,4096]{1,0:T(8,128)(2,1)}, bf16[128,4096]{1,0:T(8,128)(2,1)}, bf16[128,4096]{1,0:T(8,128)(2,1)}, f32[2,4,128,128]{3,2,1,0:T(8,128)}, f3...) custom-call(s32[2]{0:T(128)} %add_convert_fusion.1.refs_0_, ...), custom_call_target="tpu_custom_call" | custom-call | flops 80530636800 | bytes 8388608 | tf_op jit(solution)/shard_map/pallas_call | solution.py:150
  36.6 2.2 %collective-permute-start.5 = (bf16[128,4096]{1,0:T(8,128)(2,1)}, bf16[128,4096]{1,0:T(8,128)(2,1)}, u32[]{:S(2)}, u32[]{:S(2)}) collective-permute-start(bf16[128,4096]{1,0:T(8,128)(2,1)} %get-tuple-element.15), channel_id=1, source_target_pairs={{97,1},{99,3},{101,5},{103,7},{105,9},{107,11},{109,13},{111,15},{... | collective-permute-start | bytes 3145736 | tf_op jit(solution)/shard_map/ppermute | solution.py:233
  38.9 1.6 %convert_element_type.27 = f16[6,4,128,128]{3,2,1,0:T(8,128)(2,1)S(1)} convert(f32[6,4,128,128]{3,2,1,0:T(8,128)} %get-tuple-element.16) | non-fusion elementwise | flops 393216 | bytes 2359296 | tf_op jit(solution)/shard_map/convert_element_type | solution.py:289
  40.5 2.1 %collective-permute-start.6 = (f16[6,4,128,128]{3,2,1,0:T(8,128)(2,1)S(1)}, f16[6,4,128,128]{3,2,1,0:T(8,128)(2,1)S(1)}, u32[]{:S(2)}, u32[]{:S(2)}) collective-permute-start(f16[6,4,128,128]{3,2,1,0:T(8,128)(2,1)S(1)} %convert_element_type.27), channel_id=1, source_target_pairs={{0,1},{1,0},{2,3},{3,2},{4,5},{5,4},{6,7},{7,6},{8,9},{9,8},{10,11... | collective-permute-start | bytes 2359304 | tf_op jit(solution)/shard_map/ppermute | solution.py:207
  42.5 1.3 %collective-permute-start.8 = (bf16[128,4096]{1,0:T(8,128)(2,1)}, bf16[128,4096]{1,0:T(8,128)(2,1)S(1)}, u32[]{:S(2)}, u32[]{:S(2)}) collective-permute-start(bf16[128,4096]{1,0:T(8,128)(2,1)} %get-tuple-element.18), channel_id=1, source_target_pairs={{0,32},{1,33},{2,34},{3,35},{4,36},{5,37},{6,38},{7,39},{8,40},{9,... | collective-permute-start | bytes 3145736 | tf_op jit(solution)/shard_map/ppermute | solution.py:227
  43.8 4.1 %collective-permute-start.9 = (bf16[128,4096]{1,0:T(8,128)(2,1)}, bf16[128,4096]{1,0:T(8,128)(2,1)S(1)}, u32[]{:S(2)}, u32[]{:S(2)}) collective-permute-start(bf16[128,4096]{1,0:T(8,128)(2,1)} %get-tuple-element.19), channel_id=1, source_target_pairs={{32,0},{33,1},{34,2},{35,3},{36,4},{37,5},{38,6},{39,7},{40,8},{41... | collective-permute-start | bytes 3145736 | tf_op jit(solution)/shard_map/ppermute | solution.py:227
  47.9 0.0 collective-permute-done.6
  47.9 11.6 %collective-permute-done.5 = bf16[128,4096]{1,0:T(8,128)(2,1)} collective-permute-done((bf16[128,4096]{1,0:T(8,128)(2,1)}, bf16[128,4096]{1,0:T(8,128)(2,1)}, u32[]{:S(2)}, u32[]{:S(2)}) %collective-permute-start.5) | collective-permute-done | bytes 1048608 | tf_op jit(solution)/shard_map/ppermute | solution.py:233
  59.6 1.9 %collective-permute-start.7 = (bf16[128,4096]{1,0:T(8,128)(2,1)}, bf16[128,4096]{1,0:T(8,128)(2,1)S(1)}, u32[]{:S(2)}, u32[]{:S(2)}) collective-permute-start(bf16[128,4096]{1,0:T(8,128)(2,1)} %collective-permute-done.5), channel_id=1, source_target_pairs={{1,129},{3,131},{5,133},{7,135},{9,137},{11,139},{13,141},{15,143}... | collective-permute-start | bytes 3145736 | tf_op jit(solution)/shard_map/ppermute | solution.py:233
  61.5 0.3 add_convert_fusion
  61.9 1.2 %fusion.2 = (f16[2,4,128,128]{3,2,1,0:T(8,128)(2,1)S(1)}, f32[2,4,128,128]{3,2,1,0:T(8,128)}) fusion(f32[2,4,128,128]{3,2,1,0:T(8,128)S(1)} %copy-done.2, f32[2,4,128,128]{3,2,1,0:T(8,128)S(1)} %get-tuple-element.27, f32[6,4,128,128]{3,2,1,0:T(8,128)S(1)} %copy-done, pred[]{:T(512)} %eq.13, f16[6,4,128,128]{3,2,1,0:T(8,128)(2,1)S(1)} %collective-permute-done.6, ...), kind=kLoop, calls=%fused_computation.9 | loop fusion | flops 1966080 | bytes 3407873 | tf_op jit(solution)/shard_map/convert.5
  63.0 1.0 %pad_maximum_fusion = (f16[1040,128]{1,0:T(8,128)(2,1)}, f16[1040,128]{1,0:T(8,128)(2,1)}) fusion(f16[16,128]{1,0:T(8,128)(2,1)S(1)} %pad_convert_fusion, f16[1024,128]{1,0:T(8,128)(2,1)S(1)} %bitcast.15, f16[1024,128]{1,0:T(8,128)(2,1)S(1)} %bitcast.16), kind=kLoop, calls=%fused_computation.17 | loop fusion | flops 266240 | bytes 1060864 | tf_op jit(solution)/shard_map/concatenate | solution.py:202
  64.0 1.9 %collective-permute-start.11 = (f16[1040,128]{1,0:T(8,128)(2,1)}, f16[1040,128]{1,0:T(8,128)(2,1)}, u32[]{:S(2)}, u32[]{:S(2)}) collective-permute-start(f16[1040,128]{1,0:T(8,128)(2,1)} %get-tuple-element.32), channel_id=1, source_target_pairs={{2,0},{3,1},{4,2},{5,3},{6,4},{7,5},{8,6},{9,7},{10,8},{11,9},{12,... | collective-permute-start | bytes 798728 | tf_op jit(solution)/shard_map/ppermute | solution.py:212
  65.9 2.5 %collective-permute-start.10 = (f16[1040,128]{1,0:T(8,128)(2,1)}, f16[1040,128]{1,0:T(8,128)(2,1)S(1)}, u32[]{:S(2)}, u32[]{:S(2)}) collective-permute-start(f16[1040,128]{1,0:T(8,128)(2,1)} %get-tuple-element.33), channel_id=1, source_target_pairs={{4,0},{5,1},{6,2},{7,3},{8,4},{9,5},{10,6},{11,7},{12,8},{13,9},{1... | collective-permute-start | bytes 798728 | tf_op jit(solution)/shard_map/ppermute | solution.py:212
  68.4 19.3 %collective-permute-done.11 = f16[1040,128]{1,0:T(8,128)(2,1)} collective-permute-done((f16[1040,128]{1,0:T(8,128)(2,1)}, f16[1040,128]{1,0:T(8,128)(2,1)}, u32[]{:S(2)}, u32[]{:S(2)}) %collective-permute-start.11) | collective-permute-done | bytes 266272 | tf_op jit(solution)/shard_map/ppermute | solution.py:212
  87.8 1.8 %convert_element_type.32.chip_ref = f32[1040,128]{1,0:T(8,128)} convert(f16[1040,128]{1,0:T(8,128)(2,1)} %collective-permute-done.11) | non-fusion elementwise | flops 133120 | bytes 798720 | tf_op jit(solution)/shard_map/convert_element_type | solution.py:304
  89.6 0.9 convert_element_type.30.back_ref
  90.4 2.1 %shard_map.86 = (bf16[128,512]{1,0:T(8,128)(2,1)}, bf16[128,512]{1,0:T(8,128)(2,1)}) custom-call(f32[2,4,128,128]{3,2,1,0:T(8,128)} %get-tuple-element.31.own_ref, f32[1040,128]{1,0:T(8,128)} %convert_element_type.30.back_ref, f32[1040,128]{1,0:T(8,128)} %convert_element_type.32.chip_ref), custom_call_target="tpu_custom_call" | custom-call | tf_op jit(solution)/shard_map/pallas_call | solution.py:261
  92.6 1.5 %select_bitcast_fusion = (bf16[1,128,4096]{2,1,0:T(8,128)(2,1)}, bf16[1,128,4096]{2,1,0:T(8,128)(2,1)}) fusion(bf16[128,4096]{1,0:T(8,128)(2,1)S(1)} %collective-permute-done.7, bf16[128,4096]{1,0:T(8,128)(2,1)S(1)} %collective-permute-done.9, pred[]{:T(512)S(6)} %and.25, bf16[128,4096]{1,0:T(8,128)(2,1)S(1)} %collective-permute-done.8, pred[]{:T(512)S(6)} %and.24), kind=kLoop, calls=%fused_computation | loop fusion | flops 1048576 | bytes 5242882 | tf_op jit(solution)/shard_map/broadcast_in_dim | solution.py:307
  (23 shorter events, 0.1 us)
Async XLA Ops:
  2.4 11.5 %collective-permute-start.1 = (bf16[1040,128]{1,0:T(8,128)(2,1)}, bf16[1040,128]{1,0:T(8,128)(2,1)S(1)}, u32[]{:S(2)}, u32[]{:S(2)}) collective-permute-start(bf16[1040,128]{1,0:T(8,128)(2,1)} %shard_map.84.refs_3_.refs_9_.refs_15_), channel_id=1, source_target_pairs={{0,2},{1,3},{2,4},{3,5},{4,6},{5,7},{6,8},{7,9},{8,10},{9,11},{10,... | collective-permute-start | bytes 798728 | tf_op jit(solution)/shard_map/ppermute | solution.py:212
  6.4 12.1 %collective-permute-start = (bf16[1040,128]{1,0:T(8,128)(2,1)}, bf16[1040,128]{1,0:T(8,128)(2,1)S(1)}, u32[]{:S(2)}, u32[]{:S(2)}) collective-permute-start(bf16[1040,128]{1,0:T(8,128)(2,1)} %shard_map.84.refs_3_.refs_9_.refs_15_), channel_id=1, source_target_pairs={{0,4},{1,5},{2,6},{3,7},{4,8},{5,9},{6,10},{7,11},{8,12},{9,13},{1... | collective-permute-start | bytes 798728 | tf_op jit(solution)/shard_map/ppermute | solution.py:212
  8.7 12.3 %collective-permute-start.3 = (bf16[1040,128]{1,0:T(8,128)(2,1)}, bf16[1040,128]{1,0:T(8,128)(2,1)S(1)}, u32[]{:S(2)}, u32[]{:S(2)}) collective-permute-start(bf16[1040,128]{1,0:T(8,128)(2,1)} %shard_map.84.refs_3_.refs_9_.refs_15_), channel_id=1, source_target_pairs={{0,1},{1,0},{2,3},{3,2},{4,5},{5,4},{6,7},{7,6},{8,9},{9,8},{10,11... | collective-permute-start | bytes 798728 | tf_op jit(solution)/shard_map/ppermute | solution.py:207
  13.8 8.1 %copy-start.4 = (bf16[1040,128]{1,0:T(8,128)(2,1)}, bf16[1040,128]{1,0:T(8,128)(2,1)S(1)}, u32[]{:S(2)}) copy-start(bf16[1040,128]{1,0:T(8,128)(2,1)S(1)} %collective-permute-done.1.refs_5_.refs_11_.refs_17_) | copy-start | bytes 798724
  13.8 7.2 %collective-permute-start.2 = (bf16[1040,128]{1,0:T(8,128)(2,1)S(1)}, bf16[1040,128]{1,0:T(8,128)(2,1)S(1)}, u32[]{:S(2)}, u32[]{:S(2)}) collective-permute-start(bf16[1040,128]{1,0:T(8,128)(2,1)S(1)} %collective-permute-done.1.refs_5_.refs_11_.refs_17_), channel_id=1, source_target_pairs={{0,1},{1,0},{2,3},{3,2},{4,5},{5,4},{6,7},{7,6},{8,9},{9,8},{10,11... | collective-permute-start | bytes 798728 | tf_op jit(solution)/shard_map/ppermute | solution.py:207
  18.4 3.5 %copy-start.5 = (bf16[1040,128]{1,0:T(8,128)(2,1)}, bf16[1040,128]{1,0:T(8,128)(2,1)S(1)}, u32[]{:S(2)}) copy-start(bf16[1040,128]{1,0:T(8,128)(2,1)S(1)} %collective-permute-done.refs_4_.refs_10_.refs_16_) | copy-start | bytes 798724
  18.5 3.4 %collective-permute-start.4 = (bf16[1040,128]{1,0:T(8,128)(2,1)S(1)}, bf16[1040,128]{1,0:T(8,128)(2,1)S(1)}, u32[]{:S(2)}, u32[]{:S(2)}) collective-permute-start(bf16[1040,128]{1,0:T(8,128)(2,1)S(1)} %collective-permute-done.refs_4_.refs_10_.refs_16_), channel_id=1, source_target_pairs={{0,1},{1,0},{2,3},{3,2},{4,5},{5,4},{6,7},{7,6},{8,9},{9,8},{10,11... | collective-permute-start | bytes 798728 | tf_op jit(solution)/shard_map/ppermute | solution.py:207
  21.0 0.9 copy-start.6
  21.0 0.9 copy-start.7
  21.9 0.7 copy-start.8
  36.6 24.9 %copy-start = (f32[6,4,128,128]{3,2,1,0:T(8,128)S(1)}, f32[6,4,128,128]{3,2,1,0:T(8,128)}, u32[]{:S(2)}) copy-start(f32[6,4,128,128]{3,2,1,0:T(8,128)} %get-tuple-element.16) | copy-start | bytes 4718596
  36.6 24.9 %copy-start.3 = (f32[2,4,128,128]{3,2,1,0:T(8,128)S(1)}, f32[2,4,128,128]{3,2,1,0:T(8,128)}, u32[]{:S(2)}) copy-start(f32[2,4,128,128]{3,2,1,0:T(8,128)} %get-tuple-element.23) | copy-start | bytes 1572868
  36.6 22.9 %collective-permute-start.5 = (bf16[128,4096]{1,0:T(8,128)(2,1)}, bf16[128,4096]{1,0:T(8,128)(2,1)}, u32[]{:S(2)}, u32[]{:S(2)}) collective-permute-start(bf16[128,4096]{1,0:T(8,128)(2,1)} %get-tuple-element.15), channel_id=1, source_target_pairs={{97,1},{99,3},{101,5},{103,7},{105,9},{107,11},{109,13},{111,15},{... | collective-permute-start | bytes 3145736 | tf_op jit(solution)/shard_map/ppermute | solution.py:233
  40.5 21.4 %copy-start.1 = (f32[2,4,128,128]{3,2,1,0:T(8,128)S(1)}, f32[2,4,128,128]{3,2,1,0:T(8,128)}, u32[]{:S(2)}) copy-start(f32[2,4,128,128]{3,2,1,0:T(8,128)} %get-tuple-element.20) | copy-start | bytes 1572868
  40.5 21.4 %copy-start.2 = (f32[2,4,128,128]{3,2,1,0:T(8,128)S(1)}, f32[2,4,128,128]{3,2,1,0:T(8,128)}, u32[]{:S(2)}) copy-start(f32[2,4,128,128]{3,2,1,0:T(8,128)} %get-tuple-element.22) | copy-start | bytes 1572868
  40.5 7.4 %collective-permute-start.6 = (f16[6,4,128,128]{3,2,1,0:T(8,128)(2,1)S(1)}, f16[6,4,128,128]{3,2,1,0:T(8,128)(2,1)S(1)}, u32[]{:S(2)}, u32[]{:S(2)}) collective-permute-start(f16[6,4,128,128]{3,2,1,0:T(8,128)(2,1)S(1)} %convert_element_type.27), channel_id=1, source_target_pairs={{0,1},{1,0},{2,3},{3,2},{4,5},{5,4},{6,7},{7,6},{8,9},{9,8},{10,11... | collective-permute-start | bytes 2359304 | tf_op jit(solution)/shard_map/ppermute | solution.py:207
  42.5 50.0 %collective-permute-start.8 = (bf16[128,4096]{1,0:T(8,128)(2,1)}, bf16[128,4096]{1,0:T(8,128)(2,1)S(1)}, u32[]{:S(2)}, u32[]{:S(2)}) collective-permute-start(bf16[128,4096]{1,0:T(8,128)(2,1)} %get-tuple-element.18), channel_id=1, source_target_pairs={{0,32},{1,33},{2,34},{3,35},{4,36},{5,37},{6,38},{7,39},{8,40},{9,... | collective-permute-start | bytes 3145736 | tf_op jit(solution)/shard_map/ppermute | solution.py:227
  43.8 48.7 %collective-permute-start.9 = (bf16[128,4096]{1,0:T(8,128)(2,1)}, bf16[128,4096]{1,0:T(8,128)(2,1)S(1)}, u32[]{:S(2)}, u32[]{:S(2)}) collective-permute-start(bf16[128,4096]{1,0:T(8,128)(2,1)} %get-tuple-element.19), channel_id=1, source_target_pairs={{32,0},{33,1},{34,2},{35,3},{36,4},{37,5},{38,6},{39,7},{40,8},{41... | collective-permute-start | bytes 3145736 | tf_op jit(solution)/shard_map/ppermute | solution.py:227
  59.6 33.0 %collective-permute-start.7 = (bf16[128,4096]{1,0:T(8,128)(2,1)}, bf16[128,4096]{1,0:T(8,128)(2,1)S(1)}, u32[]{:S(2)}, u32[]{:S(2)}) collective-permute-start(bf16[128,4096]{1,0:T(8,128)(2,1)} %collective-permute-done.5), channel_id=1, source_target_pairs={{1,129},{3,131},{5,133},{7,135},{9,137},{11,139},{13,141},{15,143}... | collective-permute-start | bytes 3145736 | tf_op jit(solution)/shard_map/ppermute | solution.py:233
  64.0 23.7 %collective-permute-start.11 = (f16[1040,128]{1,0:T(8,128)(2,1)}, f16[1040,128]{1,0:T(8,128)(2,1)}, u32[]{:S(2)}, u32[]{:S(2)}) collective-permute-start(f16[1040,128]{1,0:T(8,128)(2,1)} %get-tuple-element.32), channel_id=1, source_target_pairs={{2,0},{3,1},{4,2},{5,3},{6,4},{7,5},{8,6},{9,7},{10,8},{11,9},{12,... | collective-permute-start | bytes 798728 | tf_op jit(solution)/shard_map/ppermute | solution.py:212
  65.9 23.6 %collective-permute-start.10 = (f16[1040,128]{1,0:T(8,128)(2,1)}, f16[1040,128]{1,0:T(8,128)(2,1)S(1)}, u32[]{:S(2)}, u32[]{:S(2)}) collective-permute-start(f16[1040,128]{1,0:T(8,128)(2,1)} %get-tuple-element.33), channel_id=1, source_target_pairs={{4,0},{5,1},{6,2},{7,3},{8,4},{9,5},{10,6},{11,7},{12,8},{13,9},{1... | collective-permute-start | bytes 798728 | tf_op jit(solution)/shard_map/ppermute | solution.py:212

commit v3 on v2

--- a/solution.py
+++ b/solution.py
@@ -213,7 +213,7 @@
 
 
 def relays(shard):
-    return shard % CHIP == 1
+    return shard % GROUP_SHARDS == 1
 
 
 def over_all(block, step):
@@ -302,8 +302,8 @@
     turned = relay(turned, legs_over(sections))
     g_own = g_own + got_near * theirs_own
     key_grads, value_grads = finish(g_own, got_back.astype(F32), got_chip.astype(F32))
-    acts_in = jnp.where(odd_core & first_in_run, turned, acts_in)
-    dq_in = jnp.where(odd_core & last_in_run, turned, dq_in)
+    acts_in = jnp.where(relays(place) & first_in_run, turned, acts_in)
+    dq_in = jnp.where(relays(place) & last_in_run, turned, dq_in)
     return acts_in[None], dq_in[None], key_grads[None], value_grads[None]
 
 

time: 94.6 us -> 102 us (1.078)
  the two profiles are of different devices: /device:TPU:167 before, /device:TPU:288 now
where the time goes in v3:
time: 102 us; the launch traced here: 101 us
  waiting for transfers between devices  39.4 us (39%)
  starting transfers between devices  33.8 us (33%)
  Pallas kernels  17.9 us (18%)
  other arithmetic  8.75 us (9%)
    ppermute x4, waiting for transfers between devices, passed_along(): lax.ppermute(block, axis, [(i - distance, i) for i in devices if i - dist...  38.9 us
    pallas_call x1, Pallas kernels, attend(): pl.pallas_call(kernel, grid=(count,), in_specs=[pl.BlockSpec(memory_space...  14 us
    ppermute x4, starting transfers between devices, swapped(): return lax.ppermute(block, 'ctx', [(i, i ^ bit) for i in devices])  11.4 us
    ppermute x2, starting transfers between devices, over_all(): return lax.ppermute(block, ('pipe', 'ctx'), route)  10.1 us
    ppermute x4, starting transfers between devices, passed_along(): lax.ppermute(block, axis, [(i - distance, i) for i in devices if i - dist...  9.78 us
    ppermute x2, starting transfers between devices, relay(): return lax.ppermute(block, ('pipe', 'ctx'), route)  2.5 us
    pallas_call x1, Pallas kernels, finish(): pl.pallas_call(finish_kernel, out_shape=[jax.ShapeDtypeStruct((ROWS, HK *...  2.12 us
  transfers between devices with their start and end apart: 12, of which 3 were waited for; matrix products, arithmetic and copies ran while one was open for 7% of the time, Pallas kernels for 2%

profile of v3, /device:TPU:288, one launch (start us, length us, event | category | flops | bytes accessed | tf_op | source)
XLA Modules:
  0.0 101.5 jit_solution(13179010887288604802)
XLA Ops:
  0.6 1.7 %shard_map.84.refs_3_.refs_9_.refs_15_ = bf16[1040,128]{1,0:T(8,128)(2,1)} custom-call(bf16[128,512]{1,0:T(8,128)(2,1)} %bitcast.17, bf16[128,512]{1,0:T(8,128)(2,1)} %bitcast.18, s32[1,128]{1,0:T(1,128)} %m_ref.1), custom_call_target="tpu_custom_call" | custom-call | tf_op jit(solution)/shard_map/pallas_call | solution.py:190
  2.4 3.4 %collective-permute-start.1 = (bf16[1040,128]{1,0:T(8,128)(2,1)}, bf16[1040,128]{1,0:T(8,128)(2,1)S(1)}, u32[]{:S(2)}, u32[]{:S(2)}) collective-permute-start(bf16[1040,128]{1,0:T(8,128)(2,1)} %shard_map.84.refs_3_.refs_9_.refs_15_), channel_id=1, source_target_pairs={{0,2},{1,3},{2,4},{3,5},{4,6},{5,7},{6,8},{7,9},{8,10},{9,11},{10,... | collective-permute-start | bytes 798728 | tf_op jit(solution)/shard_map/ppermute | solution.py:212
  5.8 2.6 %collective-permute-start = (bf16[1040,128]{1,0:T(8,128)(2,1)}, bf16[1040,128]{1,0:T(8,128)(2,1)S(1)}, u32[]{:S(2)}, u32[]{:S(2)}) collective-permute-start(bf16[1040,128]{1,0:T(8,128)(2,1)} %shard_map.84.refs_3_.refs_9_.refs_15_), channel_id=1, source_target_pairs={{0,4},{1,5},{2,6},{3,7},{4,8},{5,9},{6,10},{7,11},{8,12},{9,13},{1... | collective-permute-start | bytes 798728 | tf_op jit(solution)/shard_map/ppermute | solution.py:212
  8.3 1.9 %collective-permute-start.3 = (bf16[1040,128]{1,0:T(8,128)(2,1)}, bf16[1040,128]{1,0:T(8,128)(2,1)S(1)}, u32[]{:S(2)}, u32[]{:S(2)}) collective-permute-start(bf16[1040,128]{1,0:T(8,128)(2,1)} %shard_map.84.refs_3_.refs_9_.refs_15_), channel_id=1, source_target_pairs={{0,1},{1,0},{2,3},{3,2},{4,5},{5,4},{6,7},{7,6},{8,9},{9,8},{10,11... | collective-permute-start | bytes 798728 | tf_op jit(solution)/shard_map/ppermute | solution.py:207
  10.3 5.6 %collective-permute-done.1.refs_5_.refs_11_.refs_17_ = bf16[1040,128]{1,0:T(8,128)(2,1)S(1)} collective-permute-done((bf16[1040,128]{1,0:T(8,128)(2,1)}, bf16[1040,128]{1,0:T(8,128)(2,1)S(1)}, u32[]{:S(2)}, u32[]{:S(2)}) %collective-permute-start.1) | collective-permute-done | bytes 266272 | tf_op jit(solution)/shard_map/ppermute | solution.py:212
  15.9 1.9 %collective-permute-start.2 = (bf16[1040,128]{1,0:T(8,128)(2,1)S(1)}, bf16[1040,128]{1,0:T(8,128)(2,1)S(1)}, u32[]{:S(2)}, u32[]{:S(2)}) collective-permute-start(bf16[1040,128]{1,0:T(8,128)(2,1)S(1)} %collective-permute-done.1.refs_5_.refs_11_.refs_17_), channel_id=1, source_target_pairs={{0,1},{1,0},{2,3},{3,2},{4,5},{5,4},{6,7},{7,6},{8,9},{9,8},{10,11... | collective-permute-start | bytes 798728 | tf_op jit(solution)/shard_map/ppermute | solution.py:207
  17.8 0.0 collective-permute-done.refs_4_.refs_10_.refs_16_
  17.8 2.4 %collective-permute-start.4 = (bf16[1040,128]{1,0:T(8,128)(2,1)S(1)}, bf16[1040,128]{1,0:T(8,128)(2,1)S(1)}, u32[]{:S(2)}, u32[]{:S(2)}) collective-permute-start(bf16[1040,128]{1,0:T(8,128)(2,1)S(1)} %collective-permute-done.refs_4_.refs_10_.refs_16_), channel_id=1, source_target_pairs={{0,1},{1,0},{2,3},{3,2},{4,5},{5,4},{6,7},{7,6},{8,9},{9,8},{10,11... | collective-permute-start | bytes 798728 | tf_op jit(solution)/shard_map/ppermute | solution.py:207
  20.3 0.6 add_convert_fusion.1.refs_0_
  20.8 0.0 collective-permute-done.3.refs_7_.refs_13_.refs_19_
  20.8 0.0 collective-permute-done.2.refs_6_.refs_12_.refs_18_
  20.8 0.5 collective-permute-done.4.refs_8_.refs_14_.refs_20_
  21.4 0.2 copy-done.6
  21.5 0.1 copy-done.7
  21.6 0.4 copy-done.8
  22.1 14.0 %shard_map.85 = (bf16[128,4096]{1,0:T(8,128)(2,1)}, bf16[128,4096]{1,0:T(8,128)(2,1)}, bf16[128,4096]{1,0:T(8,128)(2,1)}, f32[2,4,128,128]{3,2,1,0:T(8,128)}, f3...) custom-call(s32[2]{0:T(128)} %add_convert_fusion.1.refs_0_, ...), custom_call_target="tpu_custom_call" | custom-call | flops 80530636800 | bytes 8388608 | tf_op jit(solution)/shard_map/pallas_call | solution.py:150
  36.1 1.8 %collective-permute-start.5 = (bf16[128,4096]{1,0:T(8,128)(2,1)}, bf16[128,4096]{1,0:T(8,128)(2,1)}, u32[]{:S(2)}, u32[]{:S(2)}) collective-permute-start(bf16[128,4096]{1,0:T(8,128)(2,1)} %get-tuple-element.15), channel_id=1, source_target_pairs={{97,1},{101,5},{105,9},{109,13},{113,17},{117,21},{121,25},{125,29... | collective-permute-start | bytes 3145736 | tf_op jit(solution)/shard_map/ppermute | solution.py:233
  37.9 1.6 %convert_element_type.27 = f16[6,4,128,128]{3,2,1,0:T(8,128)(2,1)S(1)} convert(f32[6,4,128,128]{3,2,1,0:T(8,128)} %get-tuple-element.16) | non-fusion elementwise | flops 393216 | bytes 2359296 | tf_op jit(solution)/shard_map/convert_element_type | solution.py:289
  39.5 5.2 %collective-permute-start.6 = (f16[6,4,128,128]{3,2,1,0:T(8,128)(2,1)S(1)}, f16[6,4,128,128]{3,2,1,0:T(8,128)(2,1)S(1)}, u32[]{:S(2)}, u32[]{:S(2)}) collective-permute-start(f16[6,4,128,128]{3,2,1,0:T(8,128)(2,1)S(1)} %convert_element_type.27), channel_id=1, source_target_pairs={{0,1},{1,0},{2,3},{3,2},{4,5},{5,4},{6,7},{7,6},{8,9},{9,8},{10,11... | collective-permute-start | bytes 2359304 | tf_op jit(solution)/shard_map/ppermute | solution.py:207
  44.6 1.9 %collective-permute-start.8 = (bf16[128,4096]{1,0:T(8,128)(2,1)}, bf16[128,4096]{1,0:T(8,128)(2,1)S(1)}, u32[]{:S(2)}, u32[]{:S(2)}) collective-permute-start(bf16[128,4096]{1,0:T(8,128)(2,1)} %get-tuple-element.18), channel_id=1, source_target_pairs={{0,32},{1,33},{2,34},{3,35},{4,36},{5,37},{6,38},{7,39},{8,40},{9,... | collective-permute-start | bytes 3145736 | tf_op jit(solution)/shard_map/ppermute | solution.py:227
  46.6 8.1 %collective-permute-start.9 = (bf16[128,4096]{1,0:T(8,128)(2,1)}, bf16[128,4096]{1,0:T(8,128)(2,1)S(1)}, u32[]{:S(2)}, u32[]{:S(2)}) collective-permute-start(bf16[128,4096]{1,0:T(8,128)(2,1)} %get-tuple-element.19), channel_id=1, source_target_pairs={{32,0},{33,1},{34,2},{35,3},{36,4},{37,5},{38,6},{39,7},{40,8},{41... | collective-permute-start | bytes 3145736 | tf_op jit(solution)/shard_map/ppermute | solution.py:227
  54.7 0.7 collective-permute-start.7
  55.5 0.3 add_convert_fusion
  55.9 1.2 %fusion.2 = (f16[2,4,128,128]{3,2,1,0:T(8,128)(2,1)S(1)}, f32[2,4,128,128]{3,2,1,0:T(8,128)}) fusion(f32[2,4,128,128]{3,2,1,0:T(8,128)S(1)} %copy-done.2, f32[2,4,128,128]{3,2,1,0:T(8,128)S(1)} %get-tuple-element.27, f32[6,4,128,128]{3,2,1,0:T(8,128)S(1)} %copy-done, pred[]{:T(512)} %eq.21, f16[6,4,128,128]{3,2,1,0:T(8,128)(2,1)S(1)} %collective-permute-done.6, ...), kind=kLoop, calls=%fused_computation.9 | loop fusion | flops 1966080 | bytes 3407873 | tf_op jit(solution)/shard_map/convert.5
  57.0 1.0 pad_maximum_fusion
  58.0 1.9 %collective-permute-start.11 = (f16[1040,128]{1,0:T(8,128)(2,1)}, f16[1040,128]{1,0:T(8,128)(2,1)}, u32[]{:S(2)}, u32[]{:S(2)}) collective-permute-start(f16[1040,128]{1,0:T(8,128)(2,1)} %get-tuple-element.32), channel_id=1, source_target_pairs={{2,0},{3,1},{4,2},{5,3},{6,4},{7,5},{8,6},{9,7},{10,8},{11,9},{12,... | collective-permute-start | bytes 798728 | tf_op jit(solution)/shard_map/ppermute | solution.py:212
  59.9 1.9 %collective-permute-start.10 = (f16[1040,128]{1,0:T(8,128)(2,1)}, f16[1040,128]{1,0:T(8,128)(2,1)S(1)}, u32[]{:S(2)}, u32[]{:S(2)}) collective-permute-start(f16[1040,128]{1,0:T(8,128)(2,1)} %get-tuple-element.33), channel_id=1, source_target_pairs={{4,0},{5,1},{6,2},{7,3},{8,4},{9,5},{10,6},{11,7},{12,8},{13,9},{1... | collective-permute-start | bytes 798728 | tf_op jit(solution)/shard_map/ppermute | solution.py:212
  61.9 33.3 %collective-permute-done.11 = f16[1040,128]{1,0:T(8,128)(2,1)} collective-permute-done((f16[1040,128]{1,0:T(8,128)(2,1)}, f16[1040,128]{1,0:T(8,128)(2,1)}, u32[]{:S(2)}, u32[]{:S(2)}) %collective-permute-start.11) | collective-permute-done | bytes 266272 | tf_op jit(solution)/shard_map/ppermute | solution.py:212
  95.2 1.8 %convert_element_type.32.chip_ref = f32[1040,128]{1,0:T(8,128)} convert(f16[1040,128]{1,0:T(8,128)(2,1)} %collective-permute-done.11) | non-fusion elementwise | flops 133120 | bytes 798720 | tf_op jit(solution)/shard_map/convert_element_type | solution.py:304
  97.0 0.9 convert_element_type.30.back_ref
  97.8 2.1 %shard_map.86 = (bf16[128,512]{1,0:T(8,128)(2,1)}, bf16[128,512]{1,0:T(8,128)(2,1)}) custom-call(f32[2,4,128,128]{3,2,1,0:T(8,128)} %get-tuple-element.31.own_ref, f32[1040,128]{1,0:T(8,128)} %convert_element_type.30.back_ref, f32[1040,128]{1,0:T(8,128)} %convert_element_type.32.chip_ref), custom_call_target="tpu_custom_call" | custom-call | tf_op jit(solution)/shard_map/pallas_call | solution.py:261
  100.0 1.5 %select_bitcast_fusion = (bf16[1,128,4096]{2,1,0:T(8,128)(2,1)}, bf16[1,128,4096]{2,1,0:T(8,128)(2,1)}) fusion(bf16[128,4096]{1,0:T(8,128)(2,1)S(1)} %collective-permute-done.7, bf16[128,4096]{1,0:T(8,128)(2,1)S(1)} %collective-permute-done.9, pred[]{:T(512)S(6)} %and.31, bf16[128,4096]{1,0:T(8,128)(2,1)S(1)} %collective-permute-done.8, pred[]{:T(512)S(6)} %and.29), kind=kLoop, calls=%fused_computation | loop fusion | flops 1048576 | bytes 5242882 | tf_op jit(solution)/shard_map/broadcast_in_dim | solution.py:307
  (23 shorter events, 0.1 us)
Async XLA Ops:
  2.4 13.5 %collective-permute-start.1 = (bf16[1040,128]{1,0:T(8,128)(2,1)}, bf16[1040,128]{1,0:T(8,128)(2,1)S(1)}, u32[]{:S(2)}, u32[]{:S(2)}) collective-permute-start(bf16[1040,128]{1,0:T(8,128)(2,1)} %shard_map.84.refs_3_.refs_9_.refs_15_), channel_id=1, source_target_pairs={{0,2},{1,3},{2,4},{3,5},{4,6},{5,7},{6,8},{7,9},{8,10},{9,11},{10,... | collective-permute-start | bytes 798728 | tf_op jit(solution)/shard_map/ppermute | solution.py:212
  5.8 12.0 %collective-permute-start = (bf16[1040,128]{1,0:T(8,128)(2,1)}, bf16[1040,128]{1,0:T(8,128)(2,1)S(1)}, u32[]{:S(2)}, u32[]{:S(2)}) collective-permute-start(bf16[1040,128]{1,0:T(8,128)(2,1)} %shard_map.84.refs_3_.refs_9_.refs_15_), channel_id=1, source_target_pairs={{0,4},{1,5},{2,6},{3,7},{4,8},{5,9},{6,10},{7,11},{8,12},{9,13},{1... | collective-permute-start | bytes 798728 | tf_op jit(solution)/shard_map/ppermute | solution.py:212
  8.3 12.5 %collective-permute-start.3 = (bf16[1040,128]{1,0:T(8,128)(2,1)}, bf16[1040,128]{1,0:T(8,128)(2,1)S(1)}, u32[]{:S(2)}, u32[]{:S(2)}) collective-permute-start(bf16[1040,128]{1,0:T(8,128)(2,1)} %shard_map.84.refs_3_.refs_9_.refs_15_), channel_id=1, source_target_pairs={{0,1},{1,0},{2,3},{3,2},{4,5},{5,4},{6,7},{7,6},{8,9},{9,8},{10,11... | collective-permute-start | bytes 798728 | tf_op jit(solution)/shard_map/ppermute | solution.py:207
  15.9 5.5 %copy-start.4 = (bf16[1040,128]{1,0:T(8,128)(2,1)}, bf16[1040,128]{1,0:T(8,128)(2,1)S(1)}, u32[]{:S(2)}) copy-start(bf16[1040,128]{1,0:T(8,128)(2,1)S(1)} %collective-permute-done.1.refs_5_.refs_11_.refs_17_) | copy-start | bytes 798724
  15.9 5.0 %collective-permute-start.2 = (bf16[1040,128]{1,0:T(8,128)(2,1)S(1)}, bf16[1040,128]{1,0:T(8,128)(2,1)S(1)}, u32[]{:S(2)}, u32[]{:S(2)}) collective-permute-start(bf16[1040,128]{1,0:T(8,128)(2,1)S(1)} %collective-permute-done.1.refs_5_.refs_11_.refs_17_), channel_id=1, source_target_pairs={{0,1},{1,0},{2,3},{3,2},{4,5},{5,4},{6,7},{7,6},{8,9},{9,8},{10,11... | collective-permute-start | bytes 798728 | tf_op jit(solution)/shard_map/ppermute | solution.py:207
  17.8 3.6 %copy-start.5 = (bf16[1040,128]{1,0:T(8,128)(2,1)}, bf16[1040,128]{1,0:T(8,128)(2,1)S(1)}, u32[]{:S(2)}) copy-start(bf16[1040,128]{1,0:T(8,128)(2,1)S(1)} %collective-permute-done.refs_4_.refs_10_.refs_16_) | copy-start | bytes 798724
  17.8 3.6 %collective-permute-start.4 = (bf16[1040,128]{1,0:T(8,128)(2,1)S(1)}, bf16[1040,128]{1,0:T(8,128)(2,1)S(1)}, u32[]{:S(2)}, u32[]{:S(2)}) collective-permute-start(bf16[1040,128]{1,0:T(8,128)(2,1)S(1)} %collective-permute-done.refs_4_.refs_10_.refs_16_), channel_id=1, source_target_pairs={{0,1},{1,0},{2,3},{3,2},{4,5},{5,4},{6,7},{7,6},{8,9},{9,8},{10,11... | collective-permute-start | bytes 798728 | tf_op jit(solution)/shard_map/ppermute | solution.py:207
  20.8 0.7 copy-start.6
  20.8 0.8 copy-start.7
  21.4 0.7 copy-start.8
  36.1 19.4 %copy-start = (f32[6,4,128,128]{3,2,1,0:T(8,128)S(1)}, f32[6,4,128,128]{3,2,1,0:T(8,128)}, u32[]{:S(2)}) copy-start(f32[6,4,128,128]{3,2,1,0:T(8,128)} %get-tuple-element.16) | copy-start | bytes 4718596
  36.1 19.4 %copy-start.3 = (f32[2,4,128,128]{3,2,1,0:T(8,128)S(1)}, f32[2,4,128,128]{3,2,1,0:T(8,128)}, u32[]{:S(2)}) copy-start(f32[2,4,128,128]{3,2,1,0:T(8,128)} %get-tuple-element.23) | copy-start | bytes 1572868
  36.1 18.6 %collective-permute-start.5 = (bf16[128,4096]{1,0:T(8,128)(2,1)}, bf16[128,4096]{1,0:T(8,128)(2,1)}, u32[]{:S(2)}, u32[]{:S(2)}) collective-permute-start(bf16[128,4096]{1,0:T(8,128)(2,1)} %get-tuple-element.15), channel_id=1, source_target_pairs={{97,1},{101,5},{105,9},{109,13},{113,17},{117,21},{121,25},{125,29... | collective-permute-start | bytes 3145736 | tf_op jit(solution)/shard_map/ppermute | solution.py:233
  39.4 16.4 %copy-start.1 = (f32[2,4,128,128]{3,2,1,0:T(8,128)S(1)}, f32[2,4,128,128]{3,2,1,0:T(8,128)}, u32[]{:S(2)}) copy-start(f32[2,4,128,128]{3,2,1,0:T(8,128)} %get-tuple-element.20) | copy-start | bytes 1572868
  39.5 16.4 %copy-start.2 = (f32[2,4,128,128]{3,2,1,0:T(8,128)S(1)}, f32[2,4,128,128]{3,2,1,0:T(8,128)}, u32[]{:S(2)}) copy-start(f32[2,4,128,128]{3,2,1,0:T(8,128)} %get-tuple-element.22) | copy-start | bytes 1572868
  39.5 15.3 %collective-permute-start.6 = (f16[6,4,128,128]{3,2,1,0:T(8,128)(2,1)S(1)}, f16[6,4,128,128]{3,2,1,0:T(8,128)(2,1)S(1)}, u32[]{:S(2)}, u32[]{:S(2)}) collective-permute-start(f16[6,4,128,128]{3,2,1,0:T(8,128)(2,1)S(1)} %convert_element_type.27), channel_id=1, source_target_pairs={{0,1},{1,0},{2,3},{3,2},{4,5},{5,4},{6,7},{7,6},{8,9},{9,8},{10,11... | collective-permute-start | bytes 2359304 | tf_op jit(solution)/shard_map/ppermute | solution.py:207
  44.6 55.3 %collective-permute-start.8 = (bf16[128,4096]{1,0:T(8,128)(2,1)}, bf16[128,4096]{1,0:T(8,128)(2,1)S(1)}, u32[]{:S(2)}, u32[]{:S(2)}) collective-permute-start(bf16[128,4096]{1,0:T(8,128)(2,1)} %get-tuple-element.18), channel_id=1, source_target_pairs={{0,32},{1,33},{2,34},{3,35},{4,36},{5,37},{6,38},{7,39},{8,40},{9,... | collective-permute-start | bytes 3145736 | tf_op jit(solution)/shard_map/ppermute | solution.py:227
  46.6 53.4 %collective-permute-start.9 = (bf16[128,4096]{1,0:T(8,128)(2,1)}, bf16[128,4096]{1,0:T(8,128)(2,1)S(1)}, u32[]{:S(2)}, u32[]{:S(2)}) collective-permute-start(bf16[128,4096]{1,0:T(8,128)(2,1)} %get-tuple-element.19), channel_id=1, source_target_pairs={{32,0},{33,1},{34,2},{35,3},{36,4},{37,5},{38,6},{39,7},{40,8},{41... | collective-permute-start | bytes 3145736 | tf_op jit(solution)/shard_map/ppermute | solution.py:227
  54.7 45.2 %collective-permute-start.7 = (bf16[128,4096]{1,0:T(8,128)(2,1)}, bf16[128,4096]{1,0:T(8,128)(2,1)S(1)}, u32[]{:S(2)}, u32[]{:S(2)}) collective-permute-start(bf16[128,4096]{1,0:T(8,128)(2,1)} %collective-permute-done.5), channel_id=1, source_target_pairs={{1,129},{5,133},{9,137},{13,141},{17,145},{21,149},{25,153},{29,15... | collective-permute-start | bytes 3145736 | tf_op jit(solution)/shard_map/ppermute | solution.py:233
  58.0 37.1 %collective-permute-start.11 = (f16[1040,128]{1,0:T(8,128)(2,1)}, f16[1040,128]{1,0:T(8,128)(2,1)}, u32[]{:S(2)}, u32[]{:S(2)}) collective-permute-start(f16[1040,128]{1,0:T(8,128)(2,1)} %get-tuple-element.32), channel_id=1, source_target_pairs={{2,0},{3,1},{4,2},{5,3},{6,4},{7,5},{8,6},{9,7},{10,8},{11,9},{12,... | collective-permute-start | bytes 798728 | tf_op jit(solution)/shard_map/ppermute | solution.py:212
  59.9 37.0 %collective-permute-start.10 = (f16[1040,128]{1,0:T(8,128)(2,1)}, f16[1040,128]{1,0:T(8,128)(2,1)S(1)}, u32[]{:S(2)}, u32[]{:S(2)}) collective-permute-start(f16[1040,128]{1,0:T(8,128)(2,1)} %get-tuple-element.33), channel_id=1, source_target_pairs={{4,0},{5,1},{6,2},{7,3},{8,4},{9,5},{10,6},{11,7},{12,8},{13,9},{1... | collective-permute-start | bytes 798728 | tf_op jit(solution)/shard_map/ppermute | solution.py:212
